TPU v7x, 128 devices: a whole 4x4x4 slice. The times are simulated.
128 devices in a mesh: dp: 8 (over x_lo, z), blk: 16 (over y, x_hi, core).
Axes of the slice: x: 4 (x_hi: 2, x_lo: 2; x = x_hi * 2 + x_lo), y: 4, z: 4, core: 2. Of those that a mesh axis runs over, the one named last changes fastest.
Arguments:
- query_matrix: bfloat16 [8, 3072, 4096], P('dp', 'blk'), may hold values from -6 to 6
- key_matrix: bfloat16 [8, 3072, 512], P('dp', 'blk'), may hold values from -6 to 6
- value_matrix: bfloat16 [8, 3072, 512], P('dp', 'blk'), may hold values from -6 to 6
- output_gradient: bfloat16 [8, 3072, 4096], P('dp', 'blk'), may hold values from -6 to 6
- log_softmax_norm: float32 [8, 32, 3072], P('dp', None, 'blk'), may hold values from 6 to 9
- output_dot_rows: float32 [8, 32, 3072], P('dp', None, 'blk'), may hold values from -48 to 48
- shared_prefix_keys: bfloat16 [256, 512], replicated, may hold values from -6 to 6
- shared_prefix_values: bfloat16 [256, 512], replicated, may hold values from -6 to 6
- prefix_len: int32 [8], P('dp'), may hold values from 64 to 256, as said below
- segments: int32 [8, 3072], P('dp'), may hold values from 0 to 7, never falling along the last dimension, each value on 1 to 768 neighbouring positions
- span_order: int32 [8, 32], P('dp'), may hold values from 0 to 31, each once within a row
Outputs:
- grad_query: bfloat16 [8, 3072, 4096], P('dp', 'blk')
- key_gradients: bfloat16 [8, 3072, 512], P('dp', 'blk')
- value_gradients: bfloat16 [8, 3072, 512], P('dp', 'blk')
- grad_prefix_key: float32 [256, 512], replicated
- grad_prefix_value: float32 [256, 512], replicated
Inputs may be any that keep to these rules, and one draw needn't show every extreme that they name: `prefix_len`: each pack's prefix length; at least one pack sees all 256 prefix positions. `span_order`: each pack's row is a permutation.
All inputs are finite; a program needn't handle non-finite values.
Results may differ from a plain program's by a relative error of at most 0.0049.
Values may be sent and summed in bfloat16 or wider, within the bound.
A program may use at most 128 MiB of HBM per device.

v0:
```python
import jax
import jax.numpy as jnp
from jax import lax
from jax.sharding import PartitionSpec as P

QUERY_HEADS = 32
KEY_VALUE_HEADS = 4
HEAD_WIDTH = 128


def shifted(block, axis, distance):
    devices = range(lax.axis_size(axis))
    route = [((i - distance) % len(devices), i) for i in devices]
    return lax.ppermute(block, axis, route)


def tile_grads(
    query_block, gradient_rows, softmax_norms, output_dots, key_part, value_part, visible
):
    scale = query_block.shape[-1] ** (-0.5)
    scores = (
        jnp.einsum("qhgd,khd->hgqk", query_block, key_part, preferred_element_type=jnp.float32)
        * scale
    )
    probs = jnp.where(visible[None, None], jnp.exp(scores - softmax_norms[:, :, :, None]), 0.0)
    probs_low = probs.astype(jnp.bfloat16)
    value_gradients = jnp.einsum(
        "hgqk,qhgd->khd", probs_low, gradient_rows, preferred_element_type=jnp.float32
    )
    grad_probs = jnp.einsum(
        "qhgd,khd->hgqk", gradient_rows, value_part, preferred_element_type=jnp.float32
    )
    grad_scores = (probs * (grad_probs - output_dots[:, :, :, None])).astype(jnp.bfloat16)
    grad_query = (
        jnp.einsum("hgqk,khd->qhgd", grad_scores, key_part, preferred_element_type=jnp.float32)
        * scale
    )
    key_gradients = (
        jnp.einsum("hgqk,qhgd->khd", grad_scores, query_block, preferred_element_type=jnp.float32)
        * scale
    )
    return (grad_query, key_gradients, value_gradients)


def block_grads(
    query_block, gradient_rows, softmax_norms, output_dots, key_part, value_part, visible
):
    return tile_grads(
        query_block, gradient_rows, softmax_norms, output_dots, key_part, value_part, visible
    )


def local(
    query_matrix,
    key_matrix,
    value_matrix,
    output_gradient,
    log_softmax_norm,
    output_dot_rows,
    shared_prefix_keys,
    shared_prefix_values,
    prefix_len,
    segments,
    span_order,
):
    group_width = QUERY_HEADS // KEY_VALUE_HEADS
    local_token_count = query_matrix.shape[1]
    half = local_token_count // 2
    query_block = query_matrix[0].reshape(
        local_token_count, KEY_VALUE_HEADS, group_width, HEAD_WIDTH
    )
    gradient_rows = output_gradient[0].reshape(
        local_token_count, KEY_VALUE_HEADS, group_width, HEAD_WIDTH
    )
    softmax_norms = log_softmax_norm[0].reshape(KEY_VALUE_HEADS, group_width, local_token_count)
    output_dots = output_dot_rows[0].reshape(KEY_VALUE_HEADS, group_width, local_token_count)
    local_keys = key_matrix[0].reshape(local_token_count, KEY_VALUE_HEADS, HEAD_WIDTH)
    local_values = value_matrix[0].reshape(local_token_count, KEY_VALUE_HEADS, HEAD_WIDTH)
    order = span_order[0]
    doc_ids = segments[0]
    cycle_size = lax.axis_size("blk")
    own = lax.axis_index("blk")
    offsets = jnp.arange(half, dtype=jnp.int32)

    def positions(source):
        return jnp.concatenate(
            [order[2 * source] * half + offsets, order[2 * source + 1] * half + offsets]
        )

    query_pos = positions(own)
    query_doc = doc_ids[query_pos]

    def visible_from(source):
        key_pos = positions(source)
        return (query_pos[:, None] >= key_pos[None, :]) & (
            query_doc[:, None] == doc_ids[key_pos][None, :]
        )

    blocks_home = jnp.stack([local_keys, local_values])
    gradient_sum = jnp.zeros(
        (local_token_count, KEY_VALUE_HEADS, group_width, HEAD_WIDTH), jnp.float32
    )

    def advance(index, carry):
        held, sums, total = carry
        source = (own - index) % cycle_size
        extra_q, extra_k, extra_v = block_grads(
            query_block,
            gradient_rows,
            softmax_norms,
            output_dots,
            held[0],
            held[1],
            visible_from(source),
        )
        sums = sums + jnp.stack([extra_k, extra_v])
        held = shifted(held, "blk", 1)
        sums = shifted(sums, "blk", 1)
        return (held, sums, total + extra_q)

    start = (blocks_home, jnp.zeros(blocks_home.shape, jnp.float32), gradient_sum)
    final_blocks, gradient_tiles, gradient_sum = lax.fori_loop(0, cycle_size, advance, start)
    prefix_length_count = shared_prefix_keys.shape[0]
    prefix_open = jnp.broadcast_to(
        jnp.arange(prefix_length_count, dtype=jnp.int32)[None, :] < prefix_len[0],
        (local_token_count, prefix_length_count),
    )
    prefix_q, prefix_key_block, prefix_value_block = tile_grads(
        query_block,
        gradient_rows,
        softmax_norms,
        output_dots,
        shared_prefix_keys.reshape(prefix_length_count, KEY_VALUE_HEADS, HEAD_WIDTH),
        shared_prefix_values.reshape(prefix_length_count, KEY_VALUE_HEADS, HEAD_WIDTH),
        prefix_open,
    )
    gradient_sum = gradient_sum + prefix_q
    prefix_contributions = jnp.stack([prefix_key_block, prefix_value_block]).reshape(
        2, prefix_length_count, KEY_VALUE_HEADS * HEAD_WIDTH
    )
    prefix_grads = lax.psum(prefix_contributions, ("dp", "blk"))
    grad_query = gradient_sum.reshape(1, local_token_count, QUERY_HEADS * HEAD_WIDTH).astype(
        jnp.bfloat16
    )
    key_gradients = (
        gradient_tiles[0]
        .reshape(1, local_token_count, KEY_VALUE_HEADS * HEAD_WIDTH)
        .astype(jnp.bfloat16)
    )
    value_gradients = (
        gradient_tiles[1]
        .reshape(1, local_token_count, KEY_VALUE_HEADS * HEAD_WIDTH)
        .astype(jnp.bfloat16)
    )
    return (grad_query, key_gradients, value_gradients, prefix_grads[0], prefix_grads[1])


def solution(mesh):
    return jax.shard_map(
        local,
        mesh=mesh,
        in_specs=(
            P("dp", "blk", None),
            P("dp", "blk", None),
            P("dp", "blk", None),
            P("dp", "blk", None),
            P("dp", None, "blk"),
            P("dp", None, "blk"),
            P(),
            P(),
            P("dp"),
            P("dp", None),
            P("dp", None),
        ),
        out_specs=(P("dp", "blk", None), P("dp", "blk", None), P("dp", "blk", None), P(), P()),
        check_vma=False,
    )
```

profile of v0, /device:TPU:96, one launch (start us, length us, event | category | flops | bytes accessed | tf_op | source)
XLA Modules:
  0.0 753.2 jit_solution(1900132334713330518)
XLA Ops:
  20.1 5.2 fusion.27
  44.4 690.1 %while.21 = (s32[]{:T(128)}, bf16[2,192,4,128]{3,1,2,0:T(8,128)(2,1)}, f32[2,192,4,128]{3,1,2,0:T(8,128)}, f32[192,4,8,128]{3,0,2,1:T(8,128)}, s32[192]{0:T(256)...) while((s32[]{:T(128)}, ...), condition=%wide.region_1.2_spmd.clone.clone, body=%wide.region_0.1_spmd.clone.clone.sunk | while | flops 1524709632 | bytes 64502860 | solution.py:122
  47.4 5.1 fusion.83
  54.8 5.1 fusion.86
  74.2 13.8 %collective-permute-done = bf16[2,192,4,128]{3,1,2,0:T(8,128)(2,1)} collective-permute-done((bf16[2,192,4,128]{3,1,2,0:T(8,128)(2,1)S(1)}, bf16[2,192,4,128]{3,1,2,0:T(8,128)(2,1)}, u32[]{:S(2)}, u32[]{:S(2)}) %collective-permute-start) | collective-permute-done | bytes 393248 | tf_op jit(solution)/shard_map/while/body/eval_jaxpr/ppermute | solution.py:14
  98.4 5.1 fusion.86
  117.4 13.9 %collective-permute-done = bf16[2,192,4,128]{3,1,2,0:T(8,128)(2,1)} collective-permute-done((bf16[2,192,4,128]{3,1,2,0:T(8,128)(2,1)S(1)}, bf16[2,192,4,128]{3,1,2,0:T(8,128)(2,1)}, u32[]{:S(2)}, u32[]{:S(2)}) %collective-permute-start) | collective-permute-done | bytes 393248 | tf_op jit(solution)/shard_map/while/body/eval_jaxpr/ppermute | solution.py:14
  141.7 5.1 fusion.86
  159.7 15.5 %collective-permute-done = bf16[2,192,4,128]{3,1,2,0:T(8,128)(2,1)} collective-permute-done((bf16[2,192,4,128]{3,1,2,0:T(8,128)(2,1)S(1)}, bf16[2,192,4,128]{3,1,2,0:T(8,128)(2,1)}, u32[]{:S(2)}, u32[]{:S(2)}) %collective-permute-start) | collective-permute-done | bytes 393248 | tf_op jit(solution)/shard_map/while/body/eval_jaxpr/ppermute | solution.py:14
  203.7 14.5 %collective-permute-done = bf16[2,192,4,128]{3,1,2,0:T(8,128)(2,1)} collective-permute-done((bf16[2,192,4,128]{3,1,2,0:T(8,128)(2,1)S(1)}, bf16[2,192,4,128]{3,1,2,0:T(8,128)(2,1)}, u32[]{:S(2)}, u32[]{:S(2)}) %collective-permute-start) | collective-permute-done | bytes 393248 | tf_op jit(solution)/shard_map/while/body/eval_jaxpr/ppermute | solution.py:14
  228.7 5.1 fusion.86
  246.7 14.5 %collective-permute-done = bf16[2,192,4,128]{3,1,2,0:T(8,128)(2,1)} collective-permute-done((bf16[2,192,4,128]{3,1,2,0:T(8,128)(2,1)S(1)}, bf16[2,192,4,128]{3,1,2,0:T(8,128)(2,1)}, u32[]{:S(2)}, u32[]{:S(2)}) %collective-permute-start) | collective-permute-done | bytes 393248 | tf_op jit(solution)/shard_map/while/body/eval_jaxpr/ppermute | solution.py:14
  271.7 5.1 fusion.86
  289.8 14.5 %collective-permute-done = bf16[2,192,4,128]{3,1,2,0:T(8,128)(2,1)} collective-permute-done((bf16[2,192,4,128]{3,1,2,0:T(8,128)(2,1)S(1)}, bf16[2,192,4,128]{3,1,2,0:T(8,128)(2,1)}, u32[]{:S(2)}, u32[]{:S(2)}) %collective-permute-start) | collective-permute-done | bytes 393248 | tf_op jit(solution)/shard_map/while/body/eval_jaxpr/ppermute | solution.py:14
  314.7 5.1 fusion.86
  332.8 14.5 %collective-permute-done = bf16[2,192,4,128]{3,1,2,0:T(8,128)(2,1)} collective-permute-done((bf16[2,192,4,128]{3,1,2,0:T(8,128)(2,1)S(1)}, bf16[2,192,4,128]{3,1,2,0:T(8,128)(2,1)}, u32[]{:S(2)}, u32[]{:S(2)}) %collective-permute-start) | collective-permute-done | bytes 393248 | tf_op jit(solution)/shard_map/while/body/eval_jaxpr/ppermute | solution.py:14
  357.7 5.1 fusion.86
  375.8 14.5 %collective-permute-done = bf16[2,192,4,128]{3,1,2,0:T(8,128)(2,1)} collective-permute-done((bf16[2,192,4,128]{3,1,2,0:T(8,128)(2,1)S(1)}, bf16[2,192,4,128]{3,1,2,0:T(8,128)(2,1)}, u32[]{:S(2)}, u32[]{:S(2)}) %collective-permute-start) | collective-permute-done | bytes 393248 | tf_op jit(solution)/shard_map/while/body/eval_jaxpr/ppermute | solution.py:14
  400.8 5.1 fusion.86
  418.8 14.5 %collective-permute-done = bf16[2,192,4,128]{3,1,2,0:T(8,128)(2,1)} collective-permute-done((bf16[2,192,4,128]{3,1,2,0:T(8,128)(2,1)S(1)}, bf16[2,192,4,128]{3,1,2,0:T(8,128)(2,1)}, u32[]{:S(2)}, u32[]{:S(2)}) %collective-permute-start) | collective-permute-done | bytes 393248 | tf_op jit(solution)/shard_map/while/body/eval_jaxpr/ppermute | solution.py:14
  443.8 5.1 fusion.86
  461.8 14.5 %collective-permute-done = bf16[2,192,4,128]{3,1,2,0:T(8,128)(2,1)} collective-permute-done((bf16[2,192,4,128]{3,1,2,0:T(8,128)(2,1)S(1)}, bf16[2,192,4,128]{3,1,2,0:T(8,128)(2,1)}, u32[]{:S(2)}, u32[]{:S(2)}) %collective-permute-start) | collective-permute-done | bytes 393248 | tf_op jit(solution)/shard_map/while/body/eval_jaxpr/ppermute | solution.py:14
  486.8 5.1 fusion.86
  504.8 14.5 %collective-permute-done = bf16[2,192,4,128]{3,1,2,0:T(8,128)(2,1)} collective-permute-done((bf16[2,192,4,128]{3,1,2,0:T(8,128)(2,1)S(1)}, bf16[2,192,4,128]{3,1,2,0:T(8,128)(2,1)}, u32[]{:S(2)}, u32[]{:S(2)}) %collective-permute-start) | collective-permute-done | bytes 393248 | tf_op jit(solution)/shard_map/while/body/eval_jaxpr/ppermute | solution.py:14
  529.8 5.1 fusion.86
  547.8 14.5 %collective-permute-done = bf16[2,192,4,128]{3,1,2,0:T(8,128)(2,1)} collective-permute-done((bf16[2,192,4,128]{3,1,2,0:T(8,128)(2,1)S(1)}, bf16[2,192,4,128]{3,1,2,0:T(8,128)(2,1)}, u32[]{:S(2)}, u32[]{:S(2)}) %collective-permute-start) | collective-permute-done | bytes 393248 | tf_op jit(solution)/shard_map/while/body/eval_jaxpr/ppermute | solution.py:14
  572.8 5.1 fusion.86
  590.9 14.5 %collective-permute-done = bf16[2,192,4,128]{3,1,2,0:T(8,128)(2,1)} collective-permute-done((bf16[2,192,4,128]{3,1,2,0:T(8,128)(2,1)S(1)}, bf16[2,192,4,128]{3,1,2,0:T(8,128)(2,1)}, u32[]{:S(2)}, u32[]{:S(2)}) %collective-permute-start) | collective-permute-done | bytes 393248 | tf_op jit(solution)/shard_map/while/body/eval_jaxpr/ppermute | solution.py:14
  615.8 5.1 fusion.86
  633.9 14.5 %collective-permute-done = bf16[2,192,4,128]{3,1,2,0:T(8,128)(2,1)} collective-permute-done((bf16[2,192,4,128]{3,1,2,0:T(8,128)(2,1)S(1)}, bf16[2,192,4,128]{3,1,2,0:T(8,128)(2,1)}, u32[]{:S(2)}, u32[]{:S(2)}) %collective-permute-start) | collective-permute-done | bytes 393248 | tf_op jit(solution)/shard_map/while/body/eval_jaxpr/ppermute | solution.py:14
  676.9 14.5 %collective-permute-done = bf16[2,192,4,128]{3,1,2,0:T(8,128)(2,1)} collective-permute-done((bf16[2,192,4,128]{3,1,2,0:T(8,128)(2,1)S(1)}, bf16[2,192,4,128]{3,1,2,0:T(8,128)(2,1)}, u32[]{:S(2)}, u32[]{:S(2)}) %collective-permute-start) | collective-permute-done | bytes 393248 | tf_op jit(solution)/shard_map/while/body/eval_jaxpr/ppermute | solution.py:14
  719.9 14.5 %collective-permute-done = bf16[2,192,4,128]{3,1,2,0:T(8,128)(2,1)} collective-permute-done((bf16[2,192,4,128]{3,1,2,0:T(8,128)(2,1)S(1)}, bf16[2,192,4,128]{3,1,2,0:T(8,128)(2,1)}, u32[]{:S(2)}, u32[]{:S(2)}) %collective-permute-start) | collective-permute-done | bytes 393248 | tf_op jit(solution)/shard_map/while/body/eval_jaxpr/ppermute | solution.py:14
  (363 shorter events, 407.0 us)
Async XLA Ops:
  7.2 737.0 %all-reduce.2.cloned.1.call-start = ((), (), s32[]{:S(2)}) async-start(), calls=%async_computation | async-start | bytes 2097152 | tf_op jit(solution)/shard_map/psum | solution.py:141
  67.9 20.1 %collective-permute-start.1 = (f32[2,192,4,128]{3,1,2,0:T(8,128)}, f32[2,192,4,128]{3,1,2,0:T(8,128)}, u32[]{:S(2)}, u32[]{:S(2)}) collective-permute-start(f32[2,192,4,128]{3,1,2,0:T(8,128)} %maximum_add_fusion.2), channel_id=1, source_target_pairs={{15,0},{0,1},{1,2},{2,3},{3,4},{4,5},{5,6},{6,7},{7,8},{8,9},{9,10... | collective-permute-start | bytes 2359304 | tf_op jit(solution)/shard_map/while/body/eval_jaxpr/ppermute | solution.py:14
  67.9 20.1 %collective-permute-start = (bf16[2,192,4,128]{3,1,2,0:T(8,128)(2,1)S(1)}, bf16[2,192,4,128]{3,1,2,0:T(8,128)(2,1)}, u32[]{:S(2)}, u32[]{:S(2)}) collective-permute-start(bf16[2,192,4,128]{3,1,2,0:T(8,128)(2,1)S(1)} %copy.83), channel_id=1, source_target_pairs={{15,0},{0,1},{1,2},{2,3},{3,4},{4,5},{5,6},{6,7},{7,8},{8,9},{9,10... | collective-permute-start | bytes 1179656 | tf_op jit(solution)/shard_map/while/body/eval_jaxpr/ppermute | solution.py:14
  111.5 19.8 %collective-permute-start.1 = (f32[2,192,4,128]{3,1,2,0:T(8,128)}, f32[2,192,4,128]{3,1,2,0:T(8,128)}, u32[]{:S(2)}, u32[]{:S(2)}) collective-permute-start(f32[2,192,4,128]{3,1,2,0:T(8,128)} %maximum_add_fusion.2), channel_id=1, source_target_pairs={{15,0},{0,1},{1,2},{2,3},{3,4},{4,5},{5,6},{6,7},{7,8},{8,9},{9,10... | collective-permute-start | bytes 2359304 | tf_op jit(solution)/shard_map/while/body/eval_jaxpr/ppermute | solution.py:14
  111.5 19.8 %collective-permute-start = (bf16[2,192,4,128]{3,1,2,0:T(8,128)(2,1)S(1)}, bf16[2,192,4,128]{3,1,2,0:T(8,128)(2,1)}, u32[]{:S(2)}, u32[]{:S(2)}) collective-permute-start(bf16[2,192,4,128]{3,1,2,0:T(8,128)(2,1)S(1)} %copy.83), channel_id=1, source_target_pairs={{15,0},{0,1},{1,2},{2,3},{3,4},{4,5},{5,6},{6,7},{7,8},{8,9},{9,10... | collective-permute-start | bytes 1179656 | tf_op jit(solution)/shard_map/while/body/eval_jaxpr/ppermute | solution.py:14
  154.7 20.5 %collective-permute-start.1 = (f32[2,192,4,128]{3,1,2,0:T(8,128)}, f32[2,192,4,128]{3,1,2,0:T(8,128)}, u32[]{:S(2)}, u32[]{:S(2)}) collective-permute-start(f32[2,192,4,128]{3,1,2,0:T(8,128)} %maximum_add_fusion.2), channel_id=1, source_target_pairs={{15,0},{0,1},{1,2},{2,3},{3,4},{4,5},{5,6},{6,7},{7,8},{8,9},{9,10... | collective-permute-start | bytes 2359304 | tf_op jit(solution)/shard_map/while/body/eval_jaxpr/ppermute | solution.py:14
  154.7 20.5 %collective-permute-start = (bf16[2,192,4,128]{3,1,2,0:T(8,128)(2,1)S(1)}, bf16[2,192,4,128]{3,1,2,0:T(8,128)(2,1)}, u32[]{:S(2)}, u32[]{:S(2)}) collective-permute-start(bf16[2,192,4,128]{3,1,2,0:T(8,128)(2,1)S(1)} %copy.83), channel_id=1, source_target_pairs={{15,0},{0,1},{1,2},{2,3},{3,4},{4,5},{5,6},{6,7},{7,8},{8,9},{9,10... | collective-permute-start | bytes 1179656 | tf_op jit(solution)/shard_map/while/body/eval_jaxpr/ppermute | solution.py:14
  198.7 19.6 %collective-permute-start.1 = (f32[2,192,4,128]{3,1,2,0:T(8,128)}, f32[2,192,4,128]{3,1,2,0:T(8,128)}, u32[]{:S(2)}, u32[]{:S(2)}) collective-permute-start(f32[2,192,4,128]{3,1,2,0:T(8,128)} %maximum_add_fusion.2), channel_id=1, source_target_pairs={{15,0},{0,1},{1,2},{2,3},{3,4},{4,5},{5,6},{6,7},{7,8},{8,9},{9,10... | collective-permute-start | bytes 2359304 | tf_op jit(solution)/shard_map/while/body/eval_jaxpr/ppermute | solution.py:14
  198.7 19.6 %collective-permute-start = (bf16[2,192,4,128]{3,1,2,0:T(8,128)(2,1)S(1)}, bf16[2,192,4,128]{3,1,2,0:T(8,128)(2,1)}, u32[]{:S(2)}, u32[]{:S(2)}) collective-permute-start(bf16[2,192,4,128]{3,1,2,0:T(8,128)(2,1)S(1)} %copy.83), channel_id=1, source_target_pairs={{15,0},{0,1},{1,2},{2,3},{3,4},{4,5},{5,6},{6,7},{7,8},{8,9},{9,10... | collective-permute-start | bytes 1179656 | tf_op jit(solution)/shard_map/while/body/eval_jaxpr/ppermute | solution.py:14
  241.7 19.6 %collective-permute-start.1 = (f32[2,192,4,128]{3,1,2,0:T(8,128)}, f32[2,192,4,128]{3,1,2,0:T(8,128)}, u32[]{:S(2)}, u32[]{:S(2)}) collective-permute-start(f32[2,192,4,128]{3,1,2,0:T(8,128)} %maximum_add_fusion.2), channel_id=1, source_target_pairs={{15,0},{0,1},{1,2},{2,3},{3,4},{4,5},{5,6},{6,7},{7,8},{8,9},{9,10... | collective-permute-start | bytes 2359304 | tf_op jit(solution)/shard_map/while/body/eval_jaxpr/ppermute | solution.py:14
  241.7 19.6 %collective-permute-start = (bf16[2,192,4,128]{3,1,2,0:T(8,128)(2,1)S(1)}, bf16[2,192,4,128]{3,1,2,0:T(8,128)(2,1)}, u32[]{:S(2)}, u32[]{:S(2)}) collective-permute-start(bf16[2,192,4,128]{3,1,2,0:T(8,128)(2,1)S(1)} %copy.83), channel_id=1, source_target_pairs={{15,0},{0,1},{1,2},{2,3},{3,4},{4,5},{5,6},{6,7},{7,8},{8,9},{9,10... | collective-permute-start | bytes 1179656 | tf_op jit(solution)/shard_map/while/body/eval_jaxpr/ppermute | solution.py:14
  284.8 19.6 %collective-permute-start.1 = (f32[2,192,4,128]{3,1,2,0:T(8,128)}, f32[2,192,4,128]{3,1,2,0:T(8,128)}, u32[]{:S(2)}, u32[]{:S(2)}) collective-permute-start(f32[2,192,4,128]{3,1,2,0:T(8,128)} %maximum_add_fusion.2), channel_id=1, source_target_pairs={{15,0},{0,1},{1,2},{2,3},{3,4},{4,5},{5,6},{6,7},{7,8},{8,9},{9,10... | collective-permute-start | bytes 2359304 | tf_op jit(solution)/shard_map/while/body/eval_jaxpr/ppermute | solution.py:14
  284.8 19.6 %collective-permute-start = (bf16[2,192,4,128]{3,1,2,0:T(8,128)(2,1)S(1)}, bf16[2,192,4,128]{3,1,2,0:T(8,128)(2,1)}, u32[]{:S(2)}, u32[]{:S(2)}) collective-permute-start(bf16[2,192,4,128]{3,1,2,0:T(8,128)(2,1)S(1)} %copy.83), channel_id=1, source_target_pairs={{15,0},{0,1},{1,2},{2,3},{3,4},{4,5},{5,6},{6,7},{7,8},{8,9},{9,10... | collective-permute-start | bytes 1179656 | tf_op jit(solution)/shard_map/while/body/eval_jaxpr/ppermute | solution.py:14
  327.8 19.6 %collective-permute-start.1 = (f32[2,192,4,128]{3,1,2,0:T(8,128)}, f32[2,192,4,128]{3,1,2,0:T(8,128)}, u32[]{:S(2)}, u32[]{:S(2)}) collective-permute-start(f32[2,192,4,128]{3,1,2,0:T(8,128)} %maximum_add_fusion.2), channel_id=1, source_target_pairs={{15,0},{0,1},{1,2},{2,3},{3,4},{4,5},{5,6},{6,7},{7,8},{8,9},{9,10... | collective-permute-start | bytes 2359304 | tf_op jit(solution)/shard_map/while/body/eval_jaxpr/ppermute | solution.py:14
  327.8 19.6 %collective-permute-start = (bf16[2,192,4,128]{3,1,2,0:T(8,128)(2,1)S(1)}, bf16[2,192,4,128]{3,1,2,0:T(8,128)(2,1)}, u32[]{:S(2)}, u32[]{:S(2)}) collective-permute-start(bf16[2,192,4,128]{3,1,2,0:T(8,128)(2,1)S(1)} %copy.83), channel_id=1, source_target_pairs={{15,0},{0,1},{1,2},{2,3},{3,4},{4,5},{5,6},{6,7},{7,8},{8,9},{9,10... | collective-permute-start | bytes 1179656 | tf_op jit(solution)/shard_map/while/body/eval_jaxpr/ppermute | solution.py:14
  370.8 19.6 %collective-permute-start.1 = (f32[2,192,4,128]{3,1,2,0:T(8,128)}, f32[2,192,4,128]{3,1,2,0:T(8,128)}, u32[]{:S(2)}, u32[]{:S(2)}) collective-permute-start(f32[2,192,4,128]{3,1,2,0:T(8,128)} %maximum_add_fusion.2), channel_id=1, source_target_pairs={{15,0},{0,1},{1,2},{2,3},{3,4},{4,5},{5,6},{6,7},{7,8},{8,9},{9,10... | collective-permute-start | bytes 2359304 | tf_op jit(solution)/shard_map/while/body/eval_jaxpr/ppermute | solution.py:14
  370.8 19.6 %collective-permute-start = (bf16[2,192,4,128]{3,1,2,0:T(8,128)(2,1)S(1)}, bf16[2,192,4,128]{3,1,2,0:T(8,128)(2,1)}, u32[]{:S(2)}, u32[]{:S(2)}) collective-permute-start(bf16[2,192,4,128]{3,1,2,0:T(8,128)(2,1)S(1)} %copy.83), channel_id=1, source_target_pairs={{15,0},{0,1},{1,2},{2,3},{3,4},{4,5},{5,6},{6,7},{7,8},{8,9},{9,10... | collective-permute-start | bytes 1179656 | tf_op jit(solution)/shard_map/while/body/eval_jaxpr/ppermute | solution.py:14
  413.8 19.6 %collective-permute-start.1 = (f32[2,192,4,128]{3,1,2,0:T(8,128)}, f32[2,192,4,128]{3,1,2,0:T(8,128)}, u32[]{:S(2)}, u32[]{:S(2)}) collective-permute-start(f32[2,192,4,128]{3,1,2,0:T(8,128)} %maximum_add_fusion.2), channel_id=1, source_target_pairs={{15,0},{0,1},{1,2},{2,3},{3,4},{4,5},{5,6},{6,7},{7,8},{8,9},{9,10... | collective-permute-start | bytes 2359304 | tf_op jit(solution)/shard_map/while/body/eval_jaxpr/ppermute | solution.py:14
  413.8 19.6 %collective-permute-start = (bf16[2,192,4,128]{3,1,2,0:T(8,128)(2,1)S(1)}, bf16[2,192,4,128]{3,1,2,0:T(8,128)(2,1)}, u32[]{:S(2)}, u32[]{:S(2)}) collective-permute-start(bf16[2,192,4,128]{3,1,2,0:T(8,128)(2,1)S(1)} %copy.83), channel_id=1, source_target_pairs={{15,0},{0,1},{1,2},{2,3},{3,4},{4,5},{5,6},{6,7},{7,8},{8,9},{9,10... | collective-permute-start | bytes 1179656 | tf_op jit(solution)/shard_map/while/body/eval_jaxpr/ppermute | solution.py:14
  456.8 19.6 %collective-permute-start.1 = (f32[2,192,4,128]{3,1,2,0:T(8,128)}, f32[2,192,4,128]{3,1,2,0:T(8,128)}, u32[]{:S(2)}, u32[]{:S(2)}) collective-permute-start(f32[2,192,4,128]{3,1,2,0:T(8,128)} %maximum_add_fusion.2), channel_id=1, source_target_pairs={{15,0},{0,1},{1,2},{2,3},{3,4},{4,5},{5,6},{6,7},{7,8},{8,9},{9,10... | collective-permute-start | bytes 2359304 | tf_op jit(solution)/shard_map/while/body/eval_jaxpr/ppermute | solution.py:14
  456.8 19.6 %collective-permute-start = (bf16[2,192,4,128]{3,1,2,0:T(8,128)(2,1)S(1)}, bf16[2,192,4,128]{3,1,2,0:T(8,128)(2,1)}, u32[]{:S(2)}, u32[]{:S(2)}) collective-permute-start(bf16[2,192,4,128]{3,1,2,0:T(8,128)(2,1)S(1)} %copy.83), channel_id=1, source_target_pairs={{15,0},{0,1},{1,2},{2,3},{3,4},{4,5},{5,6},{6,7},{7,8},{8,9},{9,10... | collective-permute-start | bytes 1179656 | tf_op jit(solution)/shard_map/while/body/eval_jaxpr/ppermute | solution.py:14
  499.8 19.6 %collective-permute-start.1 = (f32[2,192,4,128]{3,1,2,0:T(8,128)}, f32[2,192,4,128]{3,1,2,0:T(8,128)}, u32[]{:S(2)}, u32[]{:S(2)}) collective-permute-start(f32[2,192,4,128]{3,1,2,0:T(8,128)} %maximum_add_fusion.2), channel_id=1, source_target_pairs={{15,0},{0,1},{1,2},{2,3},{3,4},{4,5},{5,6},{6,7},{7,8},{8,9},{9,10... | collective-permute-start | bytes 2359304 | tf_op jit(solution)/shard_map/while/body/eval_jaxpr/ppermute | solution.py:14
  499.8 19.6 %collective-permute-start = (bf16[2,192,4,128]{3,1,2,0:T(8,128)(2,1)S(1)}, bf16[2,192,4,128]{3,1,2,0:T(8,128)(2,1)}, u32[]{:S(2)}, u32[]{:S(2)}) collective-permute-start(bf16[2,192,4,128]{3,1,2,0:T(8,128)(2,1)S(1)} %copy.83), channel_id=1, source_target_pairs={{15,0},{0,1},{1,2},{2,3},{3,4},{4,5},{5,6},{6,7},{7,8},{8,9},{9,10... | collective-permute-start | bytes 1179656 | tf_op jit(solution)/shard_map/while/body/eval_jaxpr/ppermute | solution.py:14
  542.8 19.6 %collective-permute-start.1 = (f32[2,192,4,128]{3,1,2,0:T(8,128)}, f32[2,192,4,128]{3,1,2,0:T(8,128)}, u32[]{:S(2)}, u32[]{:S(2)}) collective-permute-start(f32[2,192,4,128]{3,1,2,0:T(8,128)} %maximum_add_fusion.2), channel_id=1, source_target_pairs={{15,0},{0,1},{1,2},{2,3},{3,4},{4,5},{5,6},{6,7},{7,8},{8,9},{9,10... | collective-permute-start | bytes 2359304 | tf_op jit(solution)/shard_map/while/body/eval_jaxpr/ppermute | solution.py:14
  542.8 19.6 %collective-permute-start = (bf16[2,192,4,128]{3,1,2,0:T(8,128)(2,1)S(1)}, bf16[2,192,4,128]{3,1,2,0:T(8,128)(2,1)}, u32[]{:S(2)}, u32[]{:S(2)}) collective-permute-start(bf16[2,192,4,128]{3,1,2,0:T(8,128)(2,1)S(1)} %copy.83), channel_id=1, source_target_pairs={{15,0},{0,1},{1,2},{2,3},{3,4},{4,5},{5,6},{6,7},{7,8},{8,9},{9,10... | collective-permute-start | bytes 1179656 | tf_op jit(solution)/shard_map/while/body/eval_jaxpr/ppermute | solution.py:14
  585.9 19.6 %collective-permute-start.1 = (f32[2,192,4,128]{3,1,2,0:T(8,128)}, f32[2,192,4,128]{3,1,2,0:T(8,128)}, u32[]{:S(2)}, u32[]{:S(2)}) collective-permute-start(f32[2,192,4,128]{3,1,2,0:T(8,128)} %maximum_add_fusion.2), channel_id=1, source_target_pairs={{15,0},{0,1},{1,2},{2,3},{3,4},{4,5},{5,6},{6,7},{7,8},{8,9},{9,10... | collective-permute-start | bytes 2359304 | tf_op jit(solution)/shard_map/while/body/eval_jaxpr/ppermute | solution.py:14
  585.9 19.6 %collective-permute-start = (bf16[2,192,4,128]{3,1,2,0:T(8,128)(2,1)S(1)}, bf16[2,192,4,128]{3,1,2,0:T(8,128)(2,1)}, u32[]{:S(2)}, u32[]{:S(2)}) collective-permute-start(bf16[2,192,4,128]{3,1,2,0:T(8,128)(2,1)S(1)} %copy.83), channel_id=1, source_target_pairs={{15,0},{0,1},{1,2},{2,3},{3,4},{4,5},{5,6},{6,7},{7,8},{8,9},{9,10... | collective-permute-start | bytes 1179656 | tf_op jit(solution)/shard_map/while/body/eval_jaxpr/ppermute | solution.py:14
  628.9 19.6 %collective-permute-start.1 = (f32[2,192,4,128]{3,1,2,0:T(8,128)}, f32[2,192,4,128]{3,1,2,0:T(8,128)}, u32[]{:S(2)}, u32[]{:S(2)}) collective-permute-start(f32[2,192,4,128]{3,1,2,0:T(8,128)} %maximum_add_fusion.2), channel_id=1, source_target_pairs={{15,0},{0,1},{1,2},{2,3},{3,4},{4,5},{5,6},{6,7},{7,8},{8,9},{9,10... | collective-permute-start | bytes 2359304 | tf_op jit(solution)/shard_map/while/body/eval_jaxpr/ppermute | solution.py:14
  628.9 19.6 %collective-permute-start = (bf16[2,192,4,128]{3,1,2,0:T(8,128)(2,1)S(1)}, bf16[2,192,4,128]{3,1,2,0:T(8,128)(2,1)}, u32[]{:S(2)}, u32[]{:S(2)}) collective-permute-start(bf16[2,192,4,128]{3,1,2,0:T(8,128)(2,1)S(1)} %copy.83), channel_id=1, source_target_pairs={{15,0},{0,1},{1,2},{2,3},{3,4},{4,5},{5,6},{6,7},{7,8},{8,9},{9,10... | collective-permute-start | bytes 1179656 | tf_op jit(solution)/shard_map/while/body/eval_jaxpr/ppermute | solution.py:14
  671.9 19.6 %collective-permute-start.1 = (f32[2,192,4,128]{3,1,2,0:T(8,128)}, f32[2,192,4,128]{3,1,2,0:T(8,128)}, u32[]{:S(2)}, u32[]{:S(2)}) collective-permute-start(f32[2,192,4,128]{3,1,2,0:T(8,128)} %maximum_add_fusion.2), channel_id=1, source_target_pairs={{15,0},{0,1},{1,2},{2,3},{3,4},{4,5},{5,6},{6,7},{7,8},{8,9},{9,10... | collective-permute-start | bytes 2359304 | tf_op jit(solution)/shard_map/while/body/eval_jaxpr/ppermute | solution.py:14
  671.9 19.6 %collective-permute-start = (bf16[2,192,4,128]{3,1,2,0:T(8,128)(2,1)S(1)}, bf16[2,192,4,128]{3,1,2,0:T(8,128)(2,1)}, u32[]{:S(2)}, u32[]{:S(2)}) collective-permute-start(bf16[2,192,4,128]{3,1,2,0:T(8,128)(2,1)S(1)} %copy.83), channel_id=1, source_target_pairs={{15,0},{0,1},{1,2},{2,3},{3,4},{4,5},{5,6},{6,7},{7,8},{8,9},{9,10... | collective-permute-start | bytes 1179656 | tf_op jit(solution)/shard_map/while/body/eval_jaxpr/ppermute | solution.py:14
  714.9 19.6 %collective-permute-start.1 = (f32[2,192,4,128]{3,1,2,0:T(8,128)}, f32[2,192,4,128]{3,1,2,0:T(8,128)}, u32[]{:S(2)}, u32[]{:S(2)}) collective-permute-start(f32[2,192,4,128]{3,1,2,0:T(8,128)} %maximum_add_fusion.2), channel_id=1, source_target_pairs={{15,0},{0,1},{1,2},{2,3},{3,4},{4,5},{5,6},{6,7},{7,8},{8,9},{9,10... | collective-permute-start | bytes 2359304 | tf_op jit(solution)/shard_map/while/body/eval_jaxpr/ppermute | solution.py:14
  (27 other events, 136.7 us)
Sparse Core Ops, SparseCore 0:
  33.6 153.1 all-reduce.1
where the time goes:
time: 757 us; the launch traced here: 753 us
  matrix products  350 us (46%)
  waiting for transfers between devices  232 us (31%)
  local copies, waits for them, and re-layouts  74.5 us (10%)
  other arithmetic  54.9 us (7%)
  loops' own time  21.3 us (3%)
  between operations  16.2 us (2%)
    ppermute x32, waiting for transfers between devices, shifted(): return lax.ppermute(block, axis, route)  232 us
    dot_general x17, matrix products, tile_grads(): jnp.einsum('hgqk,qhgd->khd', probs_low, gradient_rows, preferred_element_...  85.3 us
    dot_general x17, matrix products, tile_grads(): jnp.einsum('qhgd,khd->hgqk', query_block, key_part, preferred_element_typ...  82.3 us
    dot_general x17, matrix products, tile_grads(): jnp.einsum('hgqk,khd->qhgd', grad_scores, key_part, preferred_element_typ...  82.1 us
    dot_general x17, matrix products, tile_grads(): jnp.einsum('qhgd,khd->hgqk', gradient_rows, value_part, preferred_element...  61.7 us
    dot_general x17, matrix products, tile_grads(): jnp.einsum('hgqk,qhgd->khd', grad_scores, query_block, preferred_element_...  38.3 us
    add x16, other arithmetic, advance(): sums = sums + jnp.stack([extra_k, extra_v])  34.1 us
    gather x16, local copies, waits for them, and re-layouts, visible_from(): doc_ids[key_pos][None, :]  23 us
  transfers between devices with their start and end apart: 33, of which 16 were waited for; matrix products, arithmetic and copies ran while one was open for 60% of the time, Pallas kernels for 0%

commit v1 on v0

v1 whole, which is shorter than its diff:
```python
import functools

import jax
import jax.numpy as jnp
from jax import lax
from jax.experimental import pallas as pl
from jax.experimental.pallas import tpu as pltpu
from jax.sharding import PartitionSpec as P

QUERY_HEADS = 32
KEY_VALUE_HEADS = 4
GROUP = QUERY_HEADS // KEY_VALUE_HEADS
WIDTH = 128
SPAN = 96
PREFIX = 256
TOKENS = 3072
SPANS = 32
CHUNK = 256
SCALE = WIDTH**-0.5
LOG2E = 1.4426950408889634
LANES = GROUP * SPAN


def nt(a, b):
    return lax.dot_general(a, b, (((1,), (1,)), ((), ())), preferred_element_type=jnp.float32)


def nn(a, b):
    return lax.dot_general(a, b, (((1,), (0,)), ((), ())), preferred_element_type=jnp.float32)


def tn(a, b):
    return lax.dot_general(a, b, (((0,), (0,)), ((), ())), preferred_element_type=jnp.float32)


def main_kernel(
    heads,
    spans,
    order_ref,
    starts_ref,
    plen_ref,
    place_ref,
    q_ref,
    g_ref,
    norm_ref,
    dot_ref,
    k_ref,
    v_ref,
    pk_ref,
    pv_ref,
    dq_ref,
    dk_ref,
    dv_ref,
    dpk_ref,
    dpv_ref,
    kcat,
    vcat,
    dkacc,
    dvacc,
):
    lane_row = lax.rem(lax.broadcasted_iota(jnp.int32, (1, LANES), 1), SPAN)
    key_row = lax.broadcasted_iota(jnp.int32, (CHUNK, 1), 0)
    prefix_seen = lax.broadcasted_iota(jnp.int32, (PREFIX, 1), 0) < plen_ref[0]

    def head_step(h, _):
        cols = pl.ds(pl.multiple_of(h * WIDTH, WIDTH), WIDTH)
        kcat[:PREFIX] = pk_ref[:, cols]
        vcat[:PREFIX] = pv_ref[:, cols]

        def reorder(t, _):
            src = pl.ds(pl.multiple_of(t * SPAN, SPAN), SPAN)
            dst = pl.ds(pl.multiple_of(PREFIX + order_ref[t] * SPAN, 32), SPAN)
            kcat[dst] = k_ref[src, cols]
            vcat[dst] = v_ref[src, cols]
            return 0

        lax.fori_loop(0, SPANS, reorder, 0)
        dkacc[...] = jnp.zeros_like(dkacc)
        dvacc[...] = jnp.zeros_like(dvacc)

        def span_step(s, _):
            rows = pl.ds(pl.multiple_of(s * SPAN, SPAN), SPAN)

            def heads_of(ref):
                return jnp.concatenate(
                    [
                        ref[rows, pl.ds(pl.multiple_of((h * GROUP + g) * WIDTH, WIDTH), WIDTH)]
                        for g in range(GROUP)
                    ],
                    axis=0,
                )

            q = heads_of(q_ref)
            grad = heads_of(g_ref)
            norm = norm_ref[s, pl.ds(h, 1), :] * LOG2E
            dot = dot_ref[s, pl.ds(h, 1), :]
            place = place_ref[s]
            upper = place * SPAN + lane_row
            lower = jnp.zeros_like(upper)
            first = jnp.int32(0)
            for d in range(8):
                start = starts_ref[d]
                lower = jnp.maximum(lower, jnp.where(start <= upper, start, 0))
                first = jnp.maximum(first, jnp.where(start <= place * SPAN, start, 0))

            def tile(keys, values, seen):
                st = nt(keys, q)
                p = jnp.where(seen, jnp.exp2(st * (SCALE * LOG2E) - norm), 0.0)
                dv = nn(p.astype(jnp.bfloat16), grad)
                dp = nt(values, grad)
                ds = (p * (dp - dot)).astype(jnp.bfloat16)
                dk = nn(ds, q)
                dq = tn(ds, keys)
                return dk, dv, dq

            dk, dv, dq = tile(kcat[:PREFIX], vcat[:PREFIX], prefix_seen)
            dkacc[:PREFIX] += dk
            dvacc[:PREFIX] += dv
            end = (place + 1) * SPAN

            def chunk_step(j, total):
                begin = end - (j + 1) * CHUNK
                at = pl.ds(pl.multiple_of(PREFIX + begin, 32), CHUNK)
                pos = begin + key_row
                seen = (pos >= lower) & (pos <= upper)
                dk, dv, dq = tile(kcat[at], vcat[at], seen)
                dkacc[at] += dk
                dvacc[at] += dv
                return total + dq

            steps = (end - first + CHUNK - 1) // CHUNK
            dq = lax.fori_loop(0, steps, chunk_step, dq)
            dq = (dq * SCALE).astype(jnp.bfloat16)
            for g in range(GROUP):
                dq_ref[rows, pl.ds(pl.multiple_of((h * GROUP + g) * WIDTH, WIDTH), WIDTH)] = dq[
                    g * SPAN : (g + 1) * SPAN
                ]
            return 0

        lax.fori_loop(0, spans, span_step, 0)
        dpk_ref[:, cols] = dkacc[:PREFIX] * SCALE
        dpv_ref[:, cols] = dvacc[:PREFIX]

        def give(t, _):
            dst = pl.ds(pl.multiple_of(t * SPAN, SPAN), SPAN)
            src = pl.ds(pl.multiple_of(PREFIX + order_ref[t] * SPAN, 32), SPAN)
            dk_ref[dst, cols] = (dkacc[src] * SCALE).astype(jnp.bfloat16)
            dv_ref[dst, cols] = dvacc[src].astype(jnp.bfloat16)
            return 0

        lax.fori_loop(0, SPANS, give, 0)
        return 0

    lax.fori_loop(0, heads, head_step, 0)


def run_main(heads, spans, order, starts, plen, place, q, g, norm, dot, k, v, pk, pv):
    smem = pl.BlockSpec(memory_space=pltpu.SMEM)
    vmem = pl.BlockSpec(memory_space=pltpu.VMEM)
    return pl.pallas_call(
        functools.partial(main_kernel, heads, spans),
        out_shape=(
            jax.ShapeDtypeStruct(q.shape, jnp.bfloat16),
            jax.ShapeDtypeStruct((TOKENS, heads * WIDTH), jnp.bfloat16),
            jax.ShapeDtypeStruct((TOKENS, heads * WIDTH), jnp.bfloat16),
            jax.ShapeDtypeStruct((PREFIX, heads * WIDTH), jnp.float32),
            jax.ShapeDtypeStruct((PREFIX, heads * WIDTH), jnp.float32),
        ),
        in_specs=[smem] * 4 + [vmem] * 8,
        out_specs=(vmem,) * 5,
        scratch_shapes=[
            pltpu.VMEM((PREFIX + TOKENS, WIDTH), jnp.bfloat16),
            pltpu.VMEM((PREFIX + TOKENS, WIDTH), jnp.bfloat16),
            pltpu.VMEM((PREFIX + TOKENS, WIDTH), jnp.float32),
            pltpu.VMEM((PREFIX + TOKENS, WIDTH), jnp.float32),
        ],
        compiler_params=pltpu.CompilerParams(vmem_limit_bytes=48 * 1024 * 1024),
    )(order, starts, plen, place, q, g, norm, dot, k, v, pk, pv)


def rows_by_span(table, heads):
    spans = table.shape[-1] // SPAN
    return (
        table.reshape(heads, GROUP, spans, SPAN).transpose(2, 0, 1, 3).reshape(spans, heads, LANES)
    )


def local(
    query_matrix,
    key_matrix,
    value_matrix,
    output_gradient,
    log_softmax_norm,
    output_dot_rows,
    shared_prefix_keys,
    shared_prefix_values,
    prefix_len,
    segments,
    span_order,
):
    order = span_order[0]
    own = lax.axis_index("blk")
    starts = jnp.sum(
        segments[0][None, :] < jnp.arange(8, dtype=jnp.int32)[:, None], axis=1, dtype=jnp.int32
    )
    place = lax.dynamic_slice(order, (2 * own,), (2,))
    keys = lax.all_gather(key_matrix[0], "blk", axis=0, tiled=True)
    values = lax.all_gather(value_matrix[0], "blk", axis=0, tiled=True)
    dq, dk, dv, dpk, dpv = run_main(
        KEY_VALUE_HEADS,
        2,
        order,
        starts,
        prefix_len,
        place,
        query_matrix[0],
        output_gradient[0],
        rows_by_span(log_softmax_norm[0], KEY_VALUE_HEADS),
        rows_by_span(output_dot_rows[0], KEY_VALUE_HEADS),
        keys,
        values,
        shared_prefix_keys,
        shared_prefix_values,
    )
    dk = lax.psum_scatter(dk, "blk", scatter_dimension=0, tiled=True)
    dv = lax.psum_scatter(dv, "blk", scatter_dimension=0, tiled=True)
    prefix = lax.psum(jnp.stack([dpk, dpv]), ("dp", "blk"))
    return dq[None], dk[None], dv[None], prefix[0], prefix[1]


def solution(mesh):
    return jax.shard_map(
        local,
        mesh=mesh,
        in_specs=(
            P("dp", "blk", None),
            P("dp", "blk", None),
            P("dp", "blk", None),
            P("dp", "blk", None),
            P("dp", None, "blk"),
            P("dp", None, "blk"),
            P(),
            P(),
            P("dp"),
            P("dp", None),
            P("dp", None),
        ),
        out_specs=(P("dp", "blk", None), P("dp", "blk", None), P("dp", "blk", None), P(), P()),
        check_vma=False,
    )
```

time: 757 us -> 474 us (0.63)
  the two profiles are of different devices: /device:TPU:96 before, /device:TPU:1 now
where the time goes in v1:
time: 474 us; the launch traced here: 473 us
  waiting for transfers between devices  415 us (88%)
  Pallas kernels  31.9 us (7%)
  between operations  14.5 us (3%)
  local copies, waits for them, and re-layouts  10.2 us (2%)
    psum x1, waiting for transfers between devices, local(): prefix = lax.psum(jnp.stack([dpk, dpv]), ('dp', 'blk'))  154 us
    reduce_scatter x1, waiting for transfers between devices, local(): dv = lax.psum_scatter(dv, 'blk', scatter_dimension=0, tiled=True)  79.1 us
    reduce_scatter x1, waiting for transfers between devices, local(): dk = lax.psum_scatter(dk, 'blk', scatter_dimension=0, tiled=True)  75.5 us
    all_gather x1, waiting for transfers between devices, local(): values = lax.all_gather(value_matrix[0], 'blk', axis=0, tiled=True)  51.9 us
    all_gather x1, waiting for transfers between devices, local(): keys = lax.all_gather(key_matrix[0], 'blk', axis=0, tiled=True)  51.9 us
    pallas_call x1, Pallas kernels, run_main(): pl.pallas_call(functools.partial(main_kernel, heads, spans), out_shape=(j...  31.9 us
  transfers between devices with their start and end apart: 5, of which 5 were waited for; matrix products, arithmetic and copies ran while one was open for 1% of the time, Pallas kernels for 0%

profile of v1, /device:TPU:1, one launch (start us, length us, event | category | flops | bytes accessed | tf_op | source)
XLA Modules:
  0.0 473.3 jit_solution(15542628794153578700)
XLA Ops:
  7.2 0.0 all-gather.5.cloned.1.call-start
  7.2 0.7 all-gather.5.cloned.1.call-update
  7.9 0.0 all-gather.7.cloned.1.call-start
  7.9 0.7 all-gather.7.cloned.1.call-update
  8.6 0.0 all-reduce.2.cloned.1.call-start
  9.3 0.8 reshape_squeeze.6
  10.2 0.1 reshape.17.norm_ref
  10.3 0.8 reshape_squeeze.7
  11.2 0.1 reshape.18.dot_ref
  11.2 0.7 dynamic-slice_bitcast_fusion.place_ref
  12.0 0.8 convert_reduce_fusion.starts_ref
  12.8 51.9 %all-gather.5.cloned.1.call-done = bf16[1,3072,512]{2,1,0:T(8,128)(2,1)} async-done(((bf16[1,192,512]{2,1,0:T(8,128)(2,1)}), bf16[1,3072,512]{2,1,0:T(8,128)(2,1)}) %all-gather.5.cloned.1.call-update) | async-done | bytes 3145744 | tf_op jit(solution)/shard_map/all_gather | solution.py:207
  64.7 51.9 %all-gather.7.cloned.1.call-done = bf16[1,3072,512]{2,1,0:T(8,128)(2,1)} async-done(((bf16[1,192,512]{2,1,0:T(8,128)(2,1)}), bf16[1,3072,512]{2,1,0:T(8,128)(2,1)}) %all-gather.7.cloned.1.call-update) | async-done | bytes 3145744 | tf_op jit(solution)/shard_map/all_gather | solution.py:208
  116.7 0.0 copy-start
  116.7 1.4 copy-done
  118.1 0.0 copy-start.1
  118.1 1.4 copy-done.1
  119.5 0.0 copy-start.2
  119.5 0.9 copy-done.2
  120.4 0.9 copy-done.3
  121.4 0.7 copy-done.4
  122.0 31.9 %shard_map.146 = (bf16[192,4096]{1,0:T(8,128)(2,1)}, bf16[3072,512]{1,0:T(8,128)(2,1)}, bf16[3072,512]{1,0:T(8,128)(2,1)}, f32[256,512]{1,0:T(8,128)S(1)}, f32[256,512]{1,0:T(8,128)S(1)}) custom-call(s32[32]{0:T(128)S(1)} %bitcast.31, s32[8]{0:T(128)S(1)} %convert_reduce_fusion.starts_ref, s32[1]{0:T(128)S(6)} %copy.25.plen_ref, ...), custom_call_target="tpu_custom_call" | custom-call | tf_op jit(solution)/shard_map/pallas_call | solution.py:160
  153.9 1.1 pad_maximum_fusion
  155.0 0.0 all-reduce.2.cloned.1.call-update
  155.1 0.0 reduce-scatter.3.cloned.1.call-start
  155.1 0.5 reduce-scatter.3.cloned.1.call-update
  155.6 0.0 reduce-scatter.5.cloned.1.call-start
  155.7 0.5 reduce-scatter.5.cloned.1.call-update
  156.2 153.6 %all-reduce.2.cloned.1.call-done = f32[2,256,512]{2,1,0:T(8,128)} async-done(((f32[2,256,512]{2,1,0:T(8,128)}), f32[2,256,512]{2,1,0:T(8,128)}) %all-reduce.2.cloned.1.call-update) | async-done | bytes 1048592 | tf_op jit(solution)/shard_map/psum | solution.py:227
  309.9 2.2 slice_bitcast_fusion
  312.1 75.5 %reduce-scatter.3.cloned.1.call-done = bf16[192,512]{1,0:T(8,128)(2,1)} async-done(((bf16[3072,512]{1,0:T(8,128)(2,1)}), bf16[192,512]{1,0:T(8,128)(2,1)}) %reduce-scatter.3.cloned.1.call-update) | async-done | bytes 196624 | tf_op jit(solution)/shard_map/reduce_scatter | solution.py:225
  387.6 79.1 %reduce-scatter.5.cloned.1.call-done = bf16[192,512]{1,0:T(8,128)(2,1)} async-done(((bf16[3072,512]{1,0:T(8,128)(2,1)}), bf16[192,512]{1,0:T(8,128)(2,1)}) %reduce-scatter.5.cloned.1.call-update) | async-done | bytes 196624 | tf_op jit(solution)/shard_map/reduce_scatter | solution.py:226
  (4 shorter events, 0.0 us)
Async XLA Ops:
  7.2 57.6 %all-gather.5.cloned.1.call-start = ((), (), s32[]{:S(2)}) async-start(), calls=%async_computation.5 | async-start | bytes 3342336 | tf_op jit(solution)/shard_map/all_gather | solution.py:207
  7.9 108.8 %all-gather.7.cloned.1.call-start = ((), (), s32[]{:S(2)}) async-start(), calls=%async_computation.6 | async-start | bytes 3342336 | tf_op jit(solution)/shard_map/all_gather | solution.py:208
  8.6 301.2 %all-reduce.2.cloned.1.call-start = ((), (), s32[]{:S(2)}) async-start(), calls=%async_computation.4 | async-start | bytes 2097152 | tf_op jit(solution)/shard_map/psum | solution.py:227
  116.7 1.4 copy-start
  118.1 1.4 copy-start.1
  119.5 0.9 copy-start.2
  120.4 0.9 copy-start.3
  121.4 0.7 copy-start.4
  155.1 232.5 %reduce-scatter.3.cloned.1.call-start = ((), (), s32[]{:S(2)}) async-start(), calls=%async_computation.2 | async-start | bytes 3342336 | tf_op jit(solution)/shard_map/reduce_scatter | solution.py:225
  155.6 311.1 %reduce-scatter.5.cloned.1.call-start = ((), (), s32[]{:S(2)}) async-start(), calls=%async_computation.3 | async-start | bytes 3342336 | tf_op jit(solution)/shard_map/reduce_scatter | solution.py:226
Sparse Core Ops, SparseCore 0:
  10.5 54.2 all-gather.4
  67.2 49.4 all-gather.6
  155.2 154.6 all-reduce.1
  314.9 72.6 reduce-scatter.2
  392.6 74.0 reduce-scatter.4

commit v2 on v1

v2 whole, which is shorter than its diff:
```python
import functools

import jax
import jax.numpy as jnp
from jax import lax
from jax.experimental import pallas as pl
from jax.experimental.pallas import tpu as pltpu
from jax.sharding import PartitionSpec as P

QUERY_HEADS = 32
KEY_VALUE_HEADS = 4
GROUP = QUERY_HEADS // KEY_VALUE_HEADS
WIDTH = 128
SPAN = 96
ROWS = 192
PREFIX = 256
TOKENS = 3072
SPANS = 32
CHUNK = 256
HEADS = 2
HALF = HEADS * GROUP * WIDTH
SCALE = WIDTH**-0.5
LOG2E = 1.4426950408889634
LANES = GROUP * SPAN
MESH = pl.DeviceIdType.MESH
BF16 = jnp.bfloat16
F32 = jnp.float32


def nt(a, b):
    return lax.dot_general(a, b, (((1,), (1,)), ((), ())), preferred_element_type=F32)


def nn(a, b):
    return lax.dot_general(a, b, (((1,), (0,)), ((), ())), preferred_element_type=F32)


def tn(a, b):
    return lax.dot_general(a, b, (((0,), (0,)), ((), ())), preferred_element_type=F32)


class Place:
    def __init__(self):
        self.dp, self.blk = lax.axis_index("dp"), lax.axis_index("blk")
        self.x_lo, self.z = self.dp // 4, lax.rem(self.dp, 4)
        self.y, self.x_hi = self.blk // 4, lax.rem(self.blk // 2, 2)
        self.core = lax.rem(self.blk, 2)
        self.x = self.x_hi * 2 + self.x_lo

    def at(self, dx=0, dy=0, dz=0, other=False):
        x = lax.rem(self.x + dx, 4)
        y = lax.rem(self.y + dy, 4)
        z = lax.rem(self.z + dz, 4)
        core = 1 - self.core if other else self.core
        return (lax.rem(x, 2) * 4 + z, (y * 2 + x // 2) * 2 + core)

    def chip(self, dy, col):
        x_hi = self.x_hi if col == 0 else 1 - self.x_hi
        return lax.rem(self.y + dy, 4) * 2 + x_hi


def meet(peers):
    barrier = pltpu.get_barrier_semaphore()
    for peer in peers:
        pl.semaphore_signal(barrier, inc=1, device_id=peer, device_id_type=MESH)
    pl.semaphore_wait(barrier, len(peers))


def remote(src, dst, send, recv, peer):
    return pltpu.make_async_remote_copy(
        src_ref=src, dst_ref=dst, send_sem=send, recv_sem=recv, device_id=peer, device_id_type=MESH
    )


def lanes(start, size):
    return pl.ds(pl.multiple_of(start, WIDTH), size)


def gather_kernel(
    q_ref,
    g_ref,
    norm_ref,
    dot_ref,
    k_ref,
    v_ref,
    qs_ref,
    gs_ref,
    norms_ref,
    dots_ref,
    kv_ref,
    local_sem,
    pair_send,
    pair_recv,
    swap_send,
    swap_recv,
    y_send,
    y_recv,
    f_send,
    f_recv,
    x_send,
    x_recv,
):
    me = Place()
    core, other = me.core, 1 - me.core
    mine = me.chip(0, 0)
    sources = (k_ref, v_ref)
    own = []
    for h in range(HEADS):
        for i in range(2):
            copy = pltpu.make_async_copy(
                sources[i].at[:, lanes((core * 2 + h) * WIDTH, WIDTH)],
                kv_ref.at[mine, core, h, i],
                local_sem.at[h, i],
            )
            copy.start()
            own.append(copy)
    sibling = me.at(other=True)
    up, down, across = me.at(dy=1), me.at(dy=3), me.at(dx=2)
    meet((sibling, up, down, across))
    sent = []

    def start(copy):
        copy.start()
        sent.append(copy)
        return copy

    pair = [
        [
            start(
                remote(
                    sources[i].at[:, lanes((other * 2 + h) * WIDTH, WIDTH)],
                    kv_ref.at[mine, core, h, i],
                    pair_send.at[h, i],
                    pair_recv.at[h, i],
                    sibling,
                )
            )
            for i in range(2)
        ]
        for h in range(HEADS)
    ]
    swaps = []
    rows16 = pl.ds(pl.multiple_of(other * 16, 16), 16)
    for n, (src, dst) in enumerate(
        (
            (q_ref.at[:, lanes(other * HALF, HALF)], qs_ref),
            (g_ref.at[:, lanes(other * HALF, HALF)], gs_ref),
            (norm_ref.at[rows16], norms_ref),
            (dot_ref.at[rows16], dots_ref),
        )
    ):
        swaps.append(remote(src, dst, swap_send.at[n], swap_recv.at[n], sibling))
    for copy in own:
        copy.wait()

    def y_pair(col, rr, h, r):
        block = kv_ref.at[me.chip(0, col), r, h]
        return [
            start(remote(block, block, y_send.at[d, col, rr, h], y_recv.at[d, col, rr, h], peer))
            for d, peer in enumerate((up, down))
        ]

    y_copies, x_copies, f_copies = {}, {}, {}
    for h in range(HEADS):
        for rr, r in enumerate((core, other)):
            if rr == 1:
                for i in range(2):
                    pair[h][i].wait_recv()
            block = kv_ref.at[mine, r, h]
            x_copies[rr, h] = start(
                remote(block, block, x_send.at[rr, h], x_recv.at[rr, h], across)
            )
            y_copies[0, rr, h] = y_pair(0, rr, h, r)
    for copy in swaps:
        start(copy)

    def forward(col, h):
        for d, (rr, dy, peer) in enumerate(((0, 3, up), (1, 1, down))):
            y_copies[col, rr, h][d].wait_recv()
            block = kv_ref.at[me.chip(dy, col), core if rr == 0 else other, h]
            f_copies[d, col, h] = start(
                remote(block, block, f_send.at[d, col, h], f_recv.at[d, col, h], peer)
            )

    for h in range(HEADS):
        for rr, r in enumerate((core, other)):
            x_copies[rr, h].wait_recv()
            y_copies[1, rr, h] = y_pair(1, rr, h, r)
        forward(0, h)
    for h in range(HEADS):
        forward(1, h)
    for col in range(2):
        for h in range(HEADS):
            y_copies[col, 1, h][0].wait_recv()
            y_copies[col, 0, h][1].wait_recv()
            f_copies[0, col, h].wait_recv()
            f_copies[1, col, h].wait_recv()
    for copy in swaps:
        copy.wait_recv()
    for copy in sent:
        copy.wait_send()


def gather(q, g, norm, dot, k, v):
    dma = pltpu.SemaphoreType.DMA
    anywhere = pl.BlockSpec(memory_space=pl.ANY)
    return pl.pallas_call(
        gather_kernel,
        out_shape=(
            jax.ShapeDtypeStruct((ROWS, HALF), BF16),
            jax.ShapeDtypeStruct((ROWS, HALF), BF16),
            jax.ShapeDtypeStruct((16, ROWS), F32),
            jax.ShapeDtypeStruct((16, ROWS), F32),
            jax.ShapeDtypeStruct((8, 2, HEADS, 2, ROWS, WIDTH), BF16),
        ),
        in_specs=[anywhere] * 6,
        out_specs=(anywhere,) * 5,
        scratch_shapes=[
            dma((HEADS, 2)),
            dma((HEADS, 2)),
            dma((HEADS, 2)),
            dma((4,)),
            dma((4,)),
            dma((2, 2, 2, HEADS)),
            dma((2, 2, 2, HEADS)),
            dma((2, 2, HEADS)),
            dma((2, 2, HEADS)),
            dma((2, HEADS)),
            dma((2, HEADS)),
        ],
        compiler_params=pltpu.CompilerParams(collective_id=0, has_side_effects=True),
        name="gather_keys",
    )(q, g, norm, dot, k, v)


def main_kernel(
    order_ref,
    starts_ref,
    plen_ref,
    q_hbm,
    g_hbm,
    qs_hbm,
    gs_hbm,
    norm_ref,
    norms_ref,
    dot_ref,
    dots_ref,
    kv_ref,
    pk_ref,
    pv_ref,
    dq_ref,
    part_ref,
    dp_ref,
    q_ref,
    g_ref,
    kcat,
    vcat,
    dkacc,
    dvacc,
    sem,
):
    blk = lax.axis_index("blk")
    core = lax.rem(blk, 2)
    chip = blk // 2
    half = lanes(core * HALF, HALF)
    copies = [
        pltpu.make_async_copy(src, dst, sem.at[n])
        for n, (src, dst) in enumerate(
            (
                (q_hbm.at[:, half], q_ref.at[0]),
                (g_hbm.at[:, half], g_ref.at[0]),
                (qs_hbm, q_ref.at[1]),
                (gs_hbm, g_ref.at[1]),
            )
        )
    ]
    for copy in copies:
        copy.start()
    lane_row = lax.rem(lax.broadcasted_iota(jnp.int32, (1, LANES), 1), SPAN)
    key_row = lax.broadcasted_iota(jnp.int32, (CHUNK, 1), 0)
    prefix_seen = lax.broadcasted_iota(jnp.int32, (PREFIX, 1), 0) < plen_ref[0]

    for copy in copies:
        copy.wait()

    for h in range(HEADS):
        cols = lanes((core * 2 + h) * WIDTH, WIDTH)
        kcat[:PREFIX] = pk_ref[:, cols]
        vcat[:PREFIX] = pv_ref[:, cols]

        def reorder(b, _):
            for half_at in range(2):
                dst = pl.ds(
                    pl.multiple_of(PREFIX + order_ref[2 * b + half_at] * SPAN, 32), SPAN
                )
                rows = pl.ds(half_at * SPAN, SPAN)
                kcat[dst] = kv_ref[b // 2, lax.rem(b, 2), h, 0, rows]
                vcat[dst] = kv_ref[b // 2, lax.rem(b, 2), h, 1, rows]
            return 0

        lax.fori_loop(0, SPANS // 2, reorder, 0)
        dkacc[...] = jnp.zeros_like(dkacc)
        dvacc[...] = jnp.zeros_like(dvacc)

        for s in range(4):
            w, r = s // 2, (s % 2) * SPAN
            rows = pl.ds(r, SPAN)

            def heads_of(ref):
                return jnp.concatenate(
                    [ref[w, rows, pl.ds((h * GROUP + g) * WIDTH, WIDTH)] for g in range(GROUP)],
                    axis=0,
                )

            def row_of(own_ref, other_ref):
                if w == 0:
                    at = pl.ds(pl.multiple_of((core * 2 + h) * GROUP, GROUP), GROUP)
                    table = own_ref[at, :][:, r : r + SPAN]
                else:
                    table = other_ref[h * GROUP : (h + 1) * GROUP, r : r + SPAN]
                return jnp.concatenate([table[g : g + 1] for g in range(GROUP)], axis=1)

            q = heads_of(q_ref)
            grad = heads_of(g_ref)
            norm = row_of(norm_ref, norms_ref) * LOG2E
            dot = row_of(dot_ref, dots_ref)
            owner = core if w == 0 else 1 - core
            place = order_ref[chip * 4 + owner * 2 + s % 2]
            upper = place * SPAN + lane_row
            lower = jnp.zeros_like(upper)
            first = jnp.int32(0)
            for d in range(8):
                start = starts_ref[d]
                lower = jnp.maximum(lower, jnp.where(start <= upper, start, 0))
                first = jnp.maximum(first, jnp.where(start <= place * SPAN, start, 0))

            def tile(keys, values, seen):
                st = nt(keys, q)
                p = jnp.where(seen, jnp.exp2(st * (SCALE * LOG2E) - norm), 0.0)
                dv = nn(p.astype(BF16), grad)
                dp = nt(values, grad)
                ds = (p * (dp - dot)).astype(BF16)
                dk = nn(ds, q)
                dq = tn(ds, keys)
                return dk, dv, dq

            dk, dv, dq = tile(kcat[:PREFIX], vcat[:PREFIX], prefix_seen)
            dkacc[:PREFIX] += dk
            dvacc[:PREFIX] += dv
            end = (place + 1) * SPAN

            def chunk_step(j, total):
                begin = end - (j + 1) * CHUNK
                at = pl.ds(pl.multiple_of(PREFIX + begin, 32), CHUNK)
                pos = begin + key_row
                seen = (pos >= lower) & (pos <= upper)
                dk, dv, dq = tile(kcat[at], vcat[at], seen)
                dkacc[at] += dk
                dvacc[at] += dv
                return total + dq

            steps = (end - first + CHUNK - 1) // CHUNK
            dq = lax.fori_loop(0, steps, chunk_step, dq)
            dq = (dq * SCALE).astype(BF16)
            for g in range(GROUP):
                dq_ref[w, rows, pl.ds((h * GROUP + g) * WIDTH, WIDTH)] = dq[
                    g * SPAN : (g + 1) * SPAN
                ]
        dp_ref[0, :, h * WIDTH : (h + 1) * WIDTH] = dkacc[:PREFIX] * SCALE
        dp_ref[1, :, h * WIDTH : (h + 1) * WIDTH] = dvacc[:PREFIX]

        def give(b, _):
            for half_at in range(2):
                src = pl.ds(
                    pl.multiple_of(PREFIX + order_ref[2 * b + half_at] * SPAN, 32), SPAN
                )
                rows = pl.ds(half_at * SPAN, SPAN)
                part_ref[b // 2, lax.rem(b, 2), h, 0, rows] = (dkacc[src] * SCALE).astype(BF16)
                part_ref[b // 2, lax.rem(b, 2), h, 1, rows] = dvacc[src].astype(BF16)
            return 0

        lax.fori_loop(0, SPANS // 2, give, 0)


def run_main(order, starts, plen, q, g, qs, gs, norm, norms, dot, dots, kv, pk, pv):
    smem = pl.BlockSpec(memory_space=pltpu.SMEM)
    vmem = pl.BlockSpec(memory_space=pltpu.VMEM)
    anywhere = pl.BlockSpec(memory_space=pl.ANY)
    return pl.pallas_call(
        main_kernel,
        out_shape=(
            jax.ShapeDtypeStruct((2, ROWS, HALF), BF16),
            jax.ShapeDtypeStruct((8, 2, HEADS, 2, ROWS, WIDTH), BF16),
            jax.ShapeDtypeStruct((2, PREFIX, HEADS * WIDTH), F32),
        ),
        in_specs=[smem] * 3 + [anywhere] * 4 + [vmem] * 7,
        out_specs=(vmem,) * 3,
        scratch_shapes=[
            pltpu.VMEM((2, ROWS, HALF), BF16),
            pltpu.VMEM((2, ROWS, HALF), BF16),
            pltpu.VMEM((PREFIX + TOKENS, WIDTH), BF16),
            pltpu.VMEM((PREFIX + TOKENS, WIDTH), BF16),
            pltpu.VMEM((PREFIX + TOKENS, WIDTH), F32),
            pltpu.VMEM((PREFIX + TOKENS, WIDTH), F32),
            pltpu.SemaphoreType.DMA((4,)),
        ],
        compiler_params=pltpu.CompilerParams(vmem_limit_bytes=48 * 1024 * 1024),
        name="tiles",
    )(order, starts, plen, q, g, qs, gs, norm, norms, dot, dots, kv, pk, pv)


def reduce_kernel(
    dq_in,
    part_ref,
    dp_ref,
    dq_ref,
    dk_ref,
    dv_ref,
    dpk_ref,
    dpv_ref,
    a_buf,
    b_buf,
    c_buf,
    c_out,
    x_buf,
    x_out,
    held,
    last_out,
    last_buf,
    z_buf,
    z_sum,
    px_buf,
    px_sum,
    py_buf,
    fin,
    fin_other,
    dq_sem,
    a_sem,
    b_sem,
    c_sem,
    x_sem,
    last_sem,
    z_sem,
    px_sem,
    py_sem,
    gx_sem,
    gz_sem,
    gc_sem,
):
    me = Place()
    core, other = me.core, 1 - me.core
    sibling = me.at(other=True)
    up, down, across = me.at(dy=1), me.at(dy=3), me.at(dx=2)
    half = lanes(core * HALF, HALF)
    keep = pltpu.make_async_copy(dq_in.at[0], dq_ref.at[:, half], dq_sem.at[2])
    keep.start()
    z_peers = [me.at(dz=d) for d in (1, 2, 3)]
    x_peers = [me.at(dx=d) for d in (1, 2, 3)]
    y_peers = [me.at(dy=d) for d in (1, 2, 3)]
    meet([sibling] + z_peers + x_peers + y_peers)
    sent = []

    def start(src, dst, sem, peer):
        copy = remote(src, dst, sem.at[0], sem.at[1], peer)
        copy.start()
        sent.append(copy)
        return copy

    far, near, mid = {}, {}, {}
    for h in range(HEADS):
        for col in (1, 0):
            for d, peer in enumerate((up, down)):
                r = 1 - d
                far[d, col, h] = start(
                    part_ref.at[me.chip(2, col), r, h],
                    a_buf.at[d, col, h],
                    a_sem.at[d, col, h],
                    peer,
                )
        for col in (1, 0):
            for d, (peer, dy) in enumerate(((up, 1), (down, 3))):
                near[d, col, h] = start(
                    part_ref.at[me.chip(dy, col), d, h],
                    b_buf.at[d, col, h],
                    b_sem.at[d, col, h],
                    peer,
                )
    z_copies = [
        start(
            dp_ref.at[:, pl.ds(pl.multiple_of(lax.rem(me.z + n + 1, 4) * 64, 64), 64)],
            z_buf.at[n],
            z_sem.at[n],
            z_peers[n],
        )
        for n in range(3)
    ]
    back = start(dq_in.at[1], dq_ref.at[:, half], dq_sem, sibling)

    def pass_on(h, col):
        for d, (peer, dy) in enumerate(((up, 1), (down, 3))):
            r = 1 - d
            far[d, col, h].wait_recv()
            c_out[d, col, h] = (
                part_ref[me.chip(dy, col), r, h].astype(F32) + a_buf[d, col, h].astype(F32)
            ).astype(BF16)
            mid[d, col, h] = start(
                c_out.at[d, col, h], c_buf.at[d, col, h], c_sem.at[d, col, h], peer
            )

    def column_sum(h, col, r):
        d = 1 - r
        mid[d, col, h].wait_recv()
        near[1 - d, col, h].wait_recv()
        return (
            part_ref[me.chip(0, col), r, h].astype(F32)
            + c_buf[d, col, h].astype(F32)
            + b_buf[1 - d, col, h].astype(F32)
        )

    x_copies = {}
    pass_on(0, 1)
    pass_on(0, 0)
    for copy in z_copies:
        copy.wait_recv()
    z_sum[...] = (
        dp_ref[:, pl.ds(pl.multiple_of(me.z * 64, 64), 64)] + z_buf[0] + z_buf[1] + z_buf[2]
    )
    px_copies = [
        start(
            z_sum.at[:, pl.ds(pl.multiple_of(lax.rem(me.x + n + 1, 4) * 16, 16), 16)],
            px_buf.at[n],
            px_sem.at[n],
            x_peers[n],
        )
        for n in range(3)
    ]
    pass_on(1, 1)
    pass_on(1, 0)

    def over_x(h):
        for r in range(2):
            x_out[r, h] = column_sum(h, 1, r).astype(BF16)
            x_copies[r, h] = start(x_out.at[r, h], x_buf.at[r, h], x_sem.at[r, h], across)

    over_x(0)
    for copy in px_copies:
        copy.wait_recv()
    piece = (
        z_sum[:, pl.ds(pl.multiple_of(me.x * 16, 16), 16)] + px_buf[0] + px_buf[1] + px_buf[2]
    )
    px_sum[...] = piece
    py_buf[me.y] = piece
    py_copies = [
        start(px_sum, py_buf.at[me.y], py_sem.at[n], y_peers[n]) for n in range(3)
    ]
    over_x(1)
    for h in range(HEADS):
        for r in range(2):
            held[r, h] = column_sum(h, 0, r)
    for copy in py_copies:
        copy.wait_recv()
    fin[me.z, me.x] = ((py_buf[0] + py_buf[1]) + py_buf[2]) + py_buf[3]
    gx_copies = [
        start(fin.at[me.z, me.x], fin.at[me.z, me.x], gx_sem.at[n], x_peers[n]) for n in range(3)
    ]
    last = {}
    for h in range(HEADS):
        for r in range(2):
            x_copies[r, h].wait_recv()
        for i in range(2):
            last_out[h, i] = (
                held[other, h, i] + x_buf[other, h, i].astype(F32)
            ).astype(BF16)
        last[h] = start(last_out.at[h], last_buf.at[h], last_sem.at[h], sibling)
    for copy in gx_copies:
        copy.wait_recv()
    gz_copies = [start(fin.at[me.z], fin.at[me.z], gz_sem.at[n], z_peers[n]) for n in range(3)]
    for h in range(HEADS):
        for i, ref in enumerate((dk_ref, dv_ref)):
            ref[:, lanes((core * 2 + h) * WIDTH, WIDTH)] = (
                held[core, h, i] + x_buf[core, h, i].astype(F32)
            ).astype(BF16)
    for copy in gz_copies:
        copy.wait_recv()
    whole = start(fin, fin_other, gc_sem, sibling)
    for h in range(HEADS):
        last[h].wait_recv()
        for i, ref in enumerate((dk_ref, dv_ref)):
            ref[:, lanes((other * 2 + h) * WIDTH, WIDTH)] = last_buf[h, i]

    def lay(src, which):
        at = lanes(which * HEADS * WIDTH, HEADS * WIDTH)
        for z in range(4):
            for x in range(4):
                rows = pl.ds(z * 64 + x * 16, 16)
                dpk_ref[rows, at] = src[z, x, 0]
                dpv_ref[rows, at] = src[z, x, 1]

    lay(fin, core)
    whole.wait_recv()
    lay(fin_other, other)
    back.wait_recv()
    keep.wait()
    for copy in sent:
        copy.wait_send()


def reduce(dq, part, dp):
    vmem = pl.BlockSpec(memory_space=pltpu.VMEM)
    anywhere = pl.BlockSpec(memory_space=pl.ANY)
    dma = pltpu.SemaphoreType.DMA
    unit = (2, ROWS, WIDTH)
    wide = HEADS * WIDTH
    return pl.pallas_call(
        reduce_kernel,
        out_shape=(
            jax.ShapeDtypeStruct((ROWS, 2 * HALF), BF16),
            jax.ShapeDtypeStruct((ROWS, 2 * wide), BF16),
            jax.ShapeDtypeStruct((ROWS, 2 * wide), BF16),
            jax.ShapeDtypeStruct((PREFIX, 2 * wide), F32),
            jax.ShapeDtypeStruct((PREFIX, 2 * wide), F32),
        ),
        in_specs=[anywhere, vmem, vmem],
        out_specs=(anywhere, vmem, vmem, vmem, vmem),
        scratch_shapes=[
            pltpu.VMEM((2, 2, HEADS) + unit, BF16),
            pltpu.VMEM((2, 2, HEADS) + unit, BF16),
            pltpu.VMEM((2, 2, HEADS) + unit, BF16),
            pltpu.VMEM((2, 2, HEADS) + unit, BF16),
            pltpu.VMEM((2, HEADS) + unit, BF16),
            pltpu.VMEM((2, HEADS) + unit, BF16),
            pltpu.VMEM((2, HEADS) + unit, F32),
            pltpu.VMEM((HEADS,) + unit, BF16),
            pltpu.VMEM((HEADS,) + unit, BF16),
            pltpu.VMEM((3, 2, 64, wide), F32),
            pltpu.VMEM((2, 64, wide), F32),
            pltpu.VMEM((3, 2, 16, wide), F32),
            pltpu.VMEM((2, 16, wide), F32),
            pltpu.VMEM((4, 2, 16, wide), F32),
            pltpu.VMEM((4, 4, 2, 16, wide), F32),
            pltpu.VMEM((4, 4, 2, 16, wide), F32),
            dma((3,)),
            dma((2, 2, HEADS, 2)),
            dma((2, 2, HEADS, 2)),
            dma((2, 2, HEADS, 2)),
            dma((2, HEADS, 2)),
            dma((HEADS, 2)),
            dma((3, 2)),
            dma((3, 2)),
            dma((3, 2)),
            dma((3, 2)),
            dma((3, 2)),
            dma((2,)),
        ],
        compiler_params=pltpu.CompilerParams(
            collective_id=1, has_side_effects=True, vmem_limit_bytes=40 * 1024 * 1024
        ),
        name="reduce_sums",
    )(dq, part, dp)


def local(
    query_matrix,
    key_matrix,
    value_matrix,
    output_gradient,
    log_softmax_norm,
    output_dot_rows,
    shared_prefix_keys,
    shared_prefix_values,
    prefix_len,
    segments,
    span_order,
):
    order = span_order[0]
    starts = jnp.sum(
        segments[0][None, :] < jnp.arange(8, dtype=jnp.int32)[:, None], axis=1, dtype=jnp.int32
    )
    q, g, norm, dot = query_matrix[0], output_gradient[0], log_softmax_norm[0], output_dot_rows[0]
    qs, gs, norms, dots, kv = gather(q, g, norm, dot, key_matrix[0], value_matrix[0])
    dq, part, dp = run_main(
        order,
        starts,
        prefix_len,
        q,
        g,
        qs,
        gs,
        norm,
        norms,
        dot,
        dots,
        kv,
        shared_prefix_keys,
        shared_prefix_values,
    )
    dq, dk, dv, dpk, dpv = reduce(dq, part, dp)
    return dq[None], dk[None], dv[None], dpk, dpv


def solution(mesh):
    return jax.shard_map(
        local,
        mesh=mesh,
        in_specs=(
            P("dp", "blk", None),
            P("dp", "blk", None),
            P("dp", "blk", None),
            P("dp", "blk", None),
            P("dp", None, "blk"),
            P("dp", None, "blk"),
            P(),
            P(),
            P("dp"),
            P("dp", None),
            P("dp", None),
        ),
        out_specs=(P("dp", "blk", None), P("dp", "blk", None), P("dp", "blk", None), P(), P()),
        check_vma=False,
    )
```

time: 474 us -> 130 us (0.27)
  waiting for transfers between devices: 415 us -> 0 us
  Pallas kernels: 31.9 us -> 117 us
  between operations: 14.5 us -> 1.41 us
    reduce_scatter x2 -> x0, waiting for transfers between devices: 155 us -> none  [the longest x1 79.1 us: local(): dv = lax.psum_scatter(dv, 'blk', scatter_dimension=0, tiled=True)]
    psum x1 -> x0, waiting for transfers between devices: 154 us -> none  [local(): prefix = lax.psum(jnp.stack([dpk, dpv]), ('dp', 'blk'))]
    all_gather x2 -> x0, waiting for transfers between devices: 104 us -> none  [the longest x1 51.9 us: local(): values = lax.all_gather(value_matrix[0], 'blk', axis=0, tiled=True)]
    pallas_call x1 -> x3, Pallas kernels: 31.9 us -> 117 us  [the longest x1 55.6 us: reduce(): pl.pallas_call(reduce_kernel, out_shape=(jax.ShapeDtypeStruct((ROWS, 2 *...]
    unnamed x10 -> x27, local copies, waits for them, and re-layouts: 5.37 us -> 9.69 us
  transfers between devices with their start and end apart: 5 -> 0, of which waited for: 5 -> 0; matrix products, arithmetic and copies ran while one was open for 1% -> 0% of each run, Pallas kernels for 0% -> 0%
where the time goes in v2:
time: 130 us; the launch traced here: 129 us
  Pallas kernels  117 us (90%)
  local copies, waits for them, and re-layouts  9.69 us (7%)
  between operations  1.41 us (1%)
    pallas_call x1, Pallas kernels, reduce(): pl.pallas_call(reduce_kernel, out_shape=(jax.ShapeDtypeStruct((ROWS, 2 *...  55.6 us
    pallas_call x1, Pallas kernels, gather(): pl.pallas_call(gather_kernel, out_shape=(jax.ShapeDtypeStruct((ROWS, HALF...  37.5 us
    pallas_call x1, Pallas kernels, run_main(): pl.pallas_call(main_kernel, out_shape=(jax.ShapeDtypeStruct((2, ROWS, HAL...  24.2 us
    unnamed x27, local copies, waits for them, and re-layouts  9.69 us

profile of v2, /device:TPU:1, one launch (start us, length us, event | category | flops | bytes accessed | tf_op | source)
XLA Modules:
  0.0 129.3 jit_solution(7470045315932899127)
XLA Ops:
  1.3 0.8 convert_reduce_fusion.starts_ref
  2.1 0.0 copy-start
  2.1 0.0 copy-start.4
  2.1 0.0 copy-start.5
  2.2 0.0 copy-start.6
  2.2 0.0 copy-start.7
  2.2 0.0 copy-start.10
  2.2 37.5 %gather_keys.1 = (bf16[192,2048]{1,0:T(8,128)(2,1)}, bf16[192,2048]{1,0:T(8,128)(2,1)}, f32[16,192]{1,0:T(8,128)}, f32[16,192]{1,0:T(8,128)}, bf16[8,2,2,2,192,128]{5,4,3,2,1,0:T(8,128)(2,1)}) custom-call(bf16[192,4096]{1,0:T(8,128)(2,1)} %bitcast.11, bf16[192,4096]{1,0:T(8,128)(2,1)} %bitcast.21, f32[32,192]{1,0:T(8,128)} %bitcast.16, f32[32,192]{1,0:T(8,128)} %bitcast.18, ...), custom_call_target="tpu_custom_call" | custom-call | tf_op jit(solution)/shard_map/gather_keys/pallas_call | solution.py:207
  39.7 0.0 copy-done
  39.7 0.0 copy-done.4
  39.7 0.0 copy-done.5
  39.7 0.0 copy-done.6
  39.7 0.0 copy-done.7
  39.8 0.0 copy-done.10
  39.8 0.0 copy-start.2
  39.8 1.1 copy-done.2
  40.9 0.0 copy-start.3
  40.9 1.1 copy-done.3
  42.0 0.0 copy-start.8
  42.0 0.7 copy-done.8
  42.7 0.0 copy-start.9
  42.7 0.7 copy-done.9
  43.5 24.2 %tiles.1 = (bf16[2,192,2048]{2,1,0:T(8,128)(2,1)S(1)}, bf16[8,2,2,2,192,128]{5,4,3,2,1,0:T(8,128)(2,1)}, f32[2,256,256]{2,1,0:T(8,128)S(1)}) custom-call(s32[32]{0:T(128)S(1)} %bitcast.20, s32[8]{0:T(128)S(1)} %convert_reduce_fusion.starts_ref, s32[1]{0:T(128)S(6)} %copy.21.plen_ref, bf16[192,4096]{1,0:T(8,128)(2,1)S(1)} %bitcast.12, ...), custom_call_target="tpu_custom_call" | custom-call | tf_op jit(solution)/shard_map/tiles/pallas_call | solution.py:389
  67.7 0.0 copy-start.1
  67.7 1.9 %copy-done.1 = bf16[8,2,2,2,192,128]{5,4,3,2,1,0:T(8,128)(2,1)S(1)} copy-done((bf16[8,2,2,2,192,128]{5,4,3,2,1,0:T(8,128)(2,1)S(1)}, bf16[8,2,2,2,192,128]{5,4,3,2,1,0:T(8,128)(2,1)}, u32[]{:S(2)}) %copy-start.1) | copy-done | bytes 3145752
  69.6 55.6 %reduce_sums.1 = (bf16[192,4096]{1,0:T(8,128)(2,1)S(1)}, bf16[192,512]{1,0:T(8,128)(2,1)S(1)}, bf16[192,512]{1,0:T(8,128)(2,1)S(1)}, f32[256,512]{1,0:T(8,128)S(1)}, f32[256,512]{1,0:T(8,128)S(1)}) custom-call(bf16[2,192,2048]{2,1,0:T(8,128)(2,1)S(1)} %get-tuple-element.23.dq_in, bf16[8,2,2,2,192,128]{5,4,3,2,1,0:T(8,128)(2,1)S(1)} %copy-done.1, ...), custom_call_target="tpu_custom_call" | custom-call | tf_op jit(solution)/shard_map/reduce_sums/pallas_call | solution.py:614
  125.2 1.1 copy.22
  126.4 0.7 copy.23
  127.1 0.7 copy.24
  127.7 0.8 copy.25
  128.5 0.8 copy.26
Async XLA Ops:
  2.1 37.6 %copy-start = (bf16[1,192,4096]{2,1,0:T(8,128)(2,1)S(1)}, bf16[1,192,4096]{2,1,0:T(8,128)(2,1)}, u32[]{:S(2)}) copy-start(bf16[1,192,4096]{2,1,0:T(8,128)(2,1)} %param.11) | copy-start | bytes 4718596
  2.1 37.6 %copy-start.4 = (bf16[256,512]{1,0:T(8,128)(2,1)S(1)}, bf16[256,512]{1,0:T(8,128)(2,1)}, u32[]{:S(2)}) copy-start(bf16[256,512]{1,0:T(8,128)(2,1)} %pk_ref.1) | copy-start | bytes 786436
  2.1 37.6 %copy-start.5 = (bf16[256,512]{1,0:T(8,128)(2,1)S(1)}, bf16[256,512]{1,0:T(8,128)(2,1)}, u32[]{:S(2)}) copy-start(bf16[256,512]{1,0:T(8,128)(2,1)} %pv_ref.1) | copy-start | bytes 786436
  2.2 37.6 %copy-start.6 = (f32[1,32,192]{2,1,0:T(8,128)S(1)}, f32[1,32,192]{2,1,0:T(8,128)}, u32[]{:S(2)}) copy-start(f32[1,32,192]{2,1,0:T(8,128)} %param.15) | copy-start | bytes 73732
  2.2 37.6 %copy-start.7 = (f32[1,32,192]{2,1,0:T(8,128)S(1)}, f32[1,32,192]{2,1,0:T(8,128)}, u32[]{:S(2)}) copy-start(f32[1,32,192]{2,1,0:T(8,128)} %param.16) | copy-start | bytes 73732
  2.2 37.6 %copy-start.10 = (s32[1,32]{1,0:T(1,128)S(1)}, s32[1,32]{1,0:T(1,128)}, u32[]{:S(2)}) copy-start(s32[1,32]{1,0:T(1,128)} %param.21) | copy-start | bytes 388
  39.8 1.1 copy-start.2
  40.9 1.1 copy-start.3
  42.0 0.7 copy-start.8
  42.7 0.7 copy-start.9
  67.7 1.9 %copy-start.1 = (bf16[8,2,2,2,192,128]{5,4,3,2,1,0:T(8,128)(2,1)S(1)}, bf16[8,2,2,2,192,128]{5,4,3,2,1,0:T(8,128)(2,1)}, u32[]{:S(2)}) copy-start(bf16[8,2,2,2,192,128]{5,4,3,2,1,0:T(8,128)(2,1)} %get-tuple-element.24.part_ref) | copy-start | bytes 9437188

commit v3 on v1

v3 whole, which is shorter than its diff:
```python
import functools

import jax
import jax.numpy as jnp
from jax import lax
from jax.experimental import pallas as pl
from jax.experimental.pallas import tpu as pltpu
from jax.sharding import PartitionSpec as P

QUERY_HEADS = 32
KEY_VALUE_HEADS = 4
GROUP = QUERY_HEADS // KEY_VALUE_HEADS
WIDTH = 128
SPAN = 96
ROWS = 192
PREFIX = 256
TOKENS = 3072
SPANS = 32
BACK = 8
REACH = BACK + 1
STARTS, PLACES, BLOCKS, HALVES, SLOTS = 0, 8, 16, 64, 128
HEADS = 2
UNITS = 2 * HEADS
HALF = HEADS * GROUP * WIDTH
SCALE = WIDTH**-0.5
LOG2E = 1.4426950408889634
LANES = GROUP * SPAN
MESH = pl.DeviceIdType.MESH
BF16 = jnp.bfloat16
F32 = jnp.float32


def nt(a, b):
    return lax.dot_general(a, b, (((1,), (1,)), ((), ())), preferred_element_type=F32)


def nn(a, b):
    return lax.dot_general(a, b, (((1,), (0,)), ((), ())), preferred_element_type=F32)


def tn(a, b):
    return lax.dot_general(a, b, (((0,), (0,)), ((), ())), preferred_element_type=F32)


class Place:
    def __init__(self):
        self.dp, self.blk = lax.axis_index("dp"), lax.axis_index("blk")
        self.x_lo, self.z = self.dp // 4, lax.rem(self.dp, 4)
        self.y, self.x_hi = self.blk // 4, lax.rem(self.blk // 2, 2)
        self.core = lax.rem(self.blk, 2)
        self.x = self.x_hi * 2 + self.x_lo

    def at(self, dx=0, dy=0, dz=0, other=False):
        x = lax.rem(self.x + dx, 4)
        y = lax.rem(self.y + dy, 4)
        z = lax.rem(self.z + dz, 4)
        core = 1 - self.core if other else self.core
        return (lax.rem(x, 2) * 4 + z, (y * 2 + x // 2) * 2 + core)

    def chip(self, dy, col):
        x_hi = self.x_hi if col == 0 else 1 - self.x_hi
        return lax.rem(self.y + dy, 4) * 2 + x_hi


def meet(peers):
    barrier = pltpu.get_barrier_semaphore()
    for peer in peers:
        pl.semaphore_signal(barrier, inc=1, device_id=peer, device_id_type=MESH)
    pl.semaphore_wait(barrier, len(peers))


def remote(src, dst, send, recv, peer):
    return pltpu.make_async_remote_copy(
        src_ref=src, dst_ref=dst, send_sem=send, recv_sem=recv, device_id=peer, device_id_type=MESH
    )


def lanes(start, size):
    return pl.ds(pl.multiple_of(start, WIDTH), size)


def prepare_kernel(order_ref, segments_ref, out_ref, inverse):
    mine = lax.axis_index("blk") // 2
    core = lax.rem(lax.axis_index("blk"), 2)
    segments = segments_ref[...]
    out_ref[STARTS] = 0
    for d in range(1, 8):
        out_ref[STARTS + d] = jnp.sum((segments < d).astype(jnp.int32))
    for t in range(SPANS):
        inverse[order_ref[t]] = t
    places = []
    for s in range(4):
        place = order_ref[mine * 4 + (core if s < 2 else 1 - core) * 2 + s % 2]
        places.append(place)
        out_ref[PLACES + s] = place
        for n in range(REACH):
            t = inverse[jnp.maximum(place - BACK + n, 0)]
            out_ref[BLOCKS + s * REACH + n] = lax.shift_right_logical(t, 1)
            out_ref[HALVES + s * REACH + n] = t & 1
    for t in range(SPANS):
        there = order_ref[t]
        for s in range(4):
            at = there - places[s] + BACK
            out_ref[SLOTS + t * 4 + s] = jnp.where((at >= 0) & (at <= BACK), at, REACH)


def prepare(order, segments):
    smem = pl.BlockSpec(memory_space=pltpu.SMEM)
    return pl.pallas_call(
        prepare_kernel,
        out_shape=jax.ShapeDtypeStruct((256,), jnp.int32),
        in_specs=[smem, pl.BlockSpec(memory_space=pltpu.VMEM)],
        out_specs=smem,
        scratch_shapes=[pltpu.SMEM((SPANS,), jnp.int32)],
        name="tables",
    )(order, segments)


def fused_kernel(
    index_ref,
    plen_ref,
    q_hbm,
    g_hbm,
    norm_hbm,
    dot_hbm,
    k_hbm,
    v_hbm,
    pk_hbm,
    pv_hbm,
    dq_ref,
    dk_ref,
    dv_ref,
    dpk_ref,
    dpv_ref,
    q_ref,
    g_ref,
    table,
    prefix,
    kv_0,
    kv_1,
    kv_2,
    kv_3,
    window,
    probs,
    slots_0,
    slots_1,
    dq_prefix,
    dq_stage,
    dp_ref,
    far_out,
    near_out,
    edge_out,
    xf_out,
    a_buf,
    b_buf,
    e_buf,
    c_buf,
    c_out,
    x_buf,
    x_out,
    xf_buf,
    held,
    last_out,
    last_buf,
    z_buf,
    z_sum,
    px_buf,
    px_sum,
    py_buf,
    fin,
    fin_other,
    load_sem,
    own_sem,
    pair_sem,
    swap_sem,
    y_sem,
    f_sem,
    gx_sem,
    gf_sem,
    keep_sem,
    back_sem,
    a_sem,
    b_sem,
    e_sem,
    c_sem,
    x_sem,
    xf_sem,
    last_sem,
    z_sem,
    px_sem,
    py_sem,
    ax_sem,
    az_sem,
    ac_sem,
):
    me = Place()
    core, other = me.core, 1 - me.core
    mine = me.chip(0, 0)
    sibling = me.at(other=True)
    up, down, across = me.at(dy=1), me.at(dy=3), me.at(dx=2)
    z_peers = [me.at(dz=d) for d in (1, 2, 3)]
    x_peers = [me.at(dx=d) for d in (1, 2, 3)]
    y_peers = [me.at(dy=d) for d in (1, 2, 3)]
    half = lanes(core * HALF, HALF)
    wide = HEADS * WIDTH
    sources, kv, slots = (k_hbm, v_hbm), (kv_0, kv_1, kv_2, kv_3), (slots_0, slots_1)
    sent = []

    def start(src, dst, sem, peer):
        copy = remote(src, dst, sem.at[0], sem.at[1], peer)
        copy.start()
        sent.append(copy)
        return copy

    def fetch(src, dst, sem):
        copy = pltpu.make_async_copy(src, dst, sem)
        copy.start()
        return copy

    def columns(u, which):
        return sources[u % 2].at[:, :, lanes((which * 2 + u // 2) * WIDTH, WIDTH)]

    own = [
        fetch(columns(u, core), kv[u].at[mine * 2 + core], own_sem.at[u]) for u in range(UNITS)
    ]
    rows16 = pl.ds(pl.multiple_of(core * 16, 16), 16)
    other16 = pl.ds(pl.multiple_of(other * 16, 16), 16)
    loads = [
        fetch(src, dst, load_sem.at[n])
        for n, (src, dst) in enumerate(
            (
                (q_hbm.at[:, half], q_ref.at[0]),
                (g_hbm.at[:, half], g_ref.at[0]),
                (norm_hbm.at[rows16], table.at[0, 0]),
                (dot_hbm.at[rows16], table.at[0, 1]),
                (pk_hbm.at[:, lanes(core * wide, wide)], prefix.at[0]),
                (pv_hbm.at[:, lanes(core * wide, wide)], prefix.at[1]),
            )
        )
    ]
    for h in range(HEADS):
        slots[h][:, :, REACH] = jnp.zeros((2, 4, SPAN, WIDTH), F32)
    meet([sibling] + z_peers + x_peers + y_peers)

    pair = [
        start(columns(u, other), kv[u].at[mine * 2 + core], pair_sem.at[u], sibling)
        for u in range(UNITS)
    ]
    for copy in own:
        copy.wait()

    y_copies, gx_copies, f_copies, gf_copies = {}, {}, {}, {}

    def y_pair(col, rr, u, r):
        block = kv[u].at[me.chip(0, col) * 2 + r]
        y_copies[col, rr, u] = [
            start(block, block, y_sem.at[d, col, rr, u], peer) for d, peer in enumerate((up, down))
        ]

    def gather_first(u):
        for rr, r in enumerate((core, other)):
            if rr == 1:
                pair[u].wait_recv()
            block = kv[u].at[mine * 2 + r]
            gx_copies[rr, u] = start(block, block, gx_sem.at[rr, u], across)
            y_pair(0, rr, u, r)

    def forward(col, u):
        for d, (rr, dy, peer) in enumerate(((0, 3, up), (1, 1, down))):
            y_copies[col, rr, u][d].wait_recv()
            block = kv[u].at[me.chip(dy, col) * 2 + (core if rr == 0 else other)]
            f_copies[d, col, u] = start(block, block, f_sem.at[d, col, u], peer)

    def gather_second(u):
        for rr, r in enumerate((core, other)):
            gx_copies[rr, u].wait_recv()
            y_pair(1, rr, u, r)
        forward(0, u)

    def gather_third(u):
        for rr, r in enumerate((core, other)):
            f_copies[rr, 0, u].wait_recv()
            block = kv[u].at[me.chip(2, 0) * 2 + r]
            gf_copies[rr, u] = start(block, block, gf_sem.at[rr, u], across)

    def gather_end(u):
        y_copies[0, 1, u][0].wait_recv()
        y_copies[0, 0, u][1].wait_recv()
        for rr in range(2):
            for d in range(2):
                y_copies[1, rr, u][d].wait_recv()
        for rr in range(2):
            gf_copies[rr, u].wait_recv()

    lane_row = lax.rem(lax.broadcasted_iota(jnp.int32, (1, LANES), 1), SPAN)
    key_row = lax.broadcasted_iota(jnp.int32, (REACH * SPAN, 1), 0)
    prefix_seen = lax.broadcasted_iota(jnp.int32, (PREFIX, 1), 0) < plen_ref[0]
    places = [index_ref[PLACES + s] for s in range(4)]

    def queries(h, s):
        w, r = s // 2, (s % 2) * SPAN

        def heads_of(ref):
            return jnp.concatenate(
                [
                    ref[w, r : r + SPAN, (h * GROUP + g) * WIDTH : (h * GROUP + g + 1) * WIDTH]
                    for g in range(GROUP)
                ],
                axis=0,
            )

        def row_of(which):
            part = table[w, which, h * GROUP : (h + 1) * GROUP, :][:, r : r + SPAN]
            return jnp.concatenate([part[g : g + 1] for g in range(GROUP)], axis=1)

        return heads_of(q_ref), heads_of(g_ref), row_of(0) * LOG2E, row_of(1)

    def tile(keys, values, seen, q, grad, norm, dot):
        st = nt(keys, q)
        p = jnp.where(seen, jnp.exp2(st * (SCALE * LOG2E) - norm), 0.0)
        dv = nn(p.astype(BF16), grad)
        dp = nt(values, grad)
        ds = (p * (dp - dot)).astype(BF16)
        dk = nn(ds, q)
        dq = tn(ds, keys)
        return dk * SCALE, dv, dq

    def prefix_tile(h, s):
        at = slice(h * WIDTH, (h + 1) * WIDTH)
        dk, dv, dq = tile(prefix[0, :, at], prefix[1, :, at], prefix_seen, *queries(h, s))
        if s == 0:
            dp_ref[0, :, at] = dk
            dp_ref[1, :, at] = dv
        else:
            dp_ref[0, :, at] += dk
            dp_ref[1, :, at] += dv
        dq_prefix[h, s] = dq

    def look(u, s):
        for n in range(REACH):
            window[u % 2, n * SPAN : (n + 1) * SPAN] = kv[u][
                index_ref[BLOCKS + s * REACH + n], index_ref[HALVES + s * REACH + n]
            ]
        return window[u % 2]

    def give_slots(h, i, s, value):
        for n in range(REACH):
            slots[h][i, s, n] = value[n * SPAN : (n + 1) * SPAN]

    def value_tile(h, s):
        q, grad, norm, dot = queries(h, s)
        upper = places[s] * SPAN + lane_row
        lower = jnp.zeros_like(upper)
        for d in range(8):
            begin = index_ref[STARTS + d]
            lower = jnp.maximum(lower, jnp.where(begin <= upper, begin, 0))
        pos = (places[s] - BACK) * SPAN + key_row
        seen = (pos >= lower) & (pos <= upper)
        st = nt(look(2 * h, s), q)
        p = jnp.where(seen, jnp.exp2(st * (SCALE * LOG2E) - norm), 0.0)
        probs[s] = p
        give_slots(h, 1, s, nn(p.astype(BF16), grad))

    def key_tile(h, s):
        w, r = s // 2, (s % 2) * SPAN
        q, grad, norm, dot = queries(h, s)
        keys = look(2 * h, s)
        dp = nt(look(2 * h + 1, s), grad)
        ds = (probs[s] * (dp - dot)).astype(BF16)
        give_slots(h, 0, s, nn(ds, q) * SCALE)
        dq = tn(ds, keys) + dq_prefix[h, s]
        dq = (dq * SCALE).astype(BF16)
        for g in range(GROUP):
            dq_stage[w, r : r + SPAN, (h * GROUP + g) * WIDTH : (h * GROUP + g + 1) * WIDTH] = dq[
                g * SPAN : (g + 1) * SPAN
            ]

    backs, keeps = [], []

    def give_dq(h):
        at = slice(h * GROUP * WIDTH, (h + 1) * GROUP * WIDTH)
        to = lanes(core * HALF + h * GROUP * WIDTH, GROUP * WIDTH)
        keeps.append(fetch(dq_stage.at[0, :, at], dq_ref.at[:, to], keep_sem.at[h]))
        backs.append(start(dq_stage.at[1, :, at], dq_ref.at[:, to], back_sem.at[h], sibling))

    def own_part(u, chip, r, n):
        total = None
        for s in range(4):
            at = index_ref[SLOTS + (chip * 4 + r * 2 + n) * 4 + s]
            term = slots[u // 2][u % 2, s, at]
            total = term if total is None else total + term
        return total

    pieces = [(n, slice(n * SPAN, (n + 1) * SPAN)) for n in range(2)]
    ways = tuple(enumerate(((up, 1), (down, 3))))
    cross, edge, near, far, mid, over, last = {}, {}, {}, {}, {}, {}, {}

    def send_cross(u):
        for r in range(2):
            for n, at in pieces:
                xf_out[r, u, at] = own_part(u, me.chip(2, 1), r, n).astype(BF16)
            cross[r, u] = start(xf_out.at[r, u], xf_buf.at[r, u], xf_sem.at[r, u], across)

    def send_edge(u):
        for r in range(2):
            for d, (peer, dy) in ways:
                for n, at in pieces:
                    edge_out[d, r, u, at] = own_part(u, me.chip(dy, 1), r, n).astype(BF16)
                edge[d, r, u] = start(
                    edge_out.at[d, r, u], e_buf.at[d, r, u], e_sem.at[d, r, u], peer
                )

    def send_near(u):
        for d, (peer, dy) in ways:
            for n, at in pieces:
                near_out[d, u, at] = own_part(u, me.chip(dy, 0), d, n).astype(BF16)
            near[d, u] = start(near_out.at[d, u], b_buf.at[d, u], b_sem.at[d, u], peer)

    def send_far(u):
        for d, (peer, dy) in ways:
            r = 1 - d
            cross[r, u].wait_recv()
            for n, at in pieces:
                far_out[d, u, at] = (
                    own_part(u, me.chip(2, 0), r, n) + xf_buf[r, u, at].astype(F32)
                ).astype(BF16)
            far[d, u] = start(far_out.at[d, u], a_buf.at[d, u], a_sem.at[d, u], peer)

    def pass_on(u):
        for d, (peer, dy) in ways:
            far[d, u].wait_recv()
            for n, at in pieces:
                c_out[d, u, at] = (
                    own_part(u, me.chip(dy, 0), 1 - d, n) + a_buf[d, u, at].astype(F32)
                ).astype(BF16)
            mid[d, u] = start(c_out.at[d, u], c_buf.at[d, u], c_sem.at[d, u], peer)

    def over_x(u):
        for r in range(2):
            for d in range(2):
                edge[d, r, u].wait_recv()
            for n, at in pieces:
                x_out[r, u, at] = (
                    own_part(u, me.chip(0, 1), r, n)
                    + e_buf[0, r, u, at].astype(F32)
                    + e_buf[1, r, u, at].astype(F32)
                ).astype(BF16)
            over[r, u] = start(x_out.at[r, u], x_buf.at[r, u], x_sem.at[r, u], across)

    def hold(u):
        for r in range(2):
            d = 1 - r
            mid[d, u].wait_recv()
            near[1 - d, u].wait_recv()
            for n, at in pieces:
                held[r, u, at] = (
                    own_part(u, mine, r, n)
                    + c_buf[d, u, at].astype(F32)
                    + b_buf[1 - d, u, at].astype(F32)
                )

    def finish(u):
        for r in range(2):
            over[r, u].wait_recv()
        last_out[u] = (held[other, u] + x_buf[other, u].astype(F32)).astype(BF16)
        last[u] = start(last_out.at[u], last_buf.at[u], last_sem.at[u], sibling)
        ref = (dk_ref, dv_ref)[u % 2]
        ref[:, lanes((core * 2 + u // 2) * WIDTH, WIDTH)] = (
            held[core, u] + x_buf[core, u].astype(F32)
        ).astype(BF16)

    def take_last(u):
        last[u].wait_recv()
        ref = (dk_ref, dv_ref)[u % 2]
        ref[:, lanes((other * 2 + u // 2) * WIDTH, WIDTH)] = last_buf[u]

    def reduce_first(u):
        send_cross(u)
        send_edge(u)
        send_near(u)

    def reduce_second(u):
        send_far(u)
        over_x(u)

    def reduce_last(u):
        hold(u)
        finish(u)

    def sixteen(i, size):
        return pl.ds(pl.multiple_of(i * size, size), size)

    steps = {}

    def prefix_z():
        steps["z"] = [
            start(dp_ref.at[:, sixteen(lax.rem(me.z + n + 1, 4), 64)], z_buf.at[n], z_sem.at[n], p)
            for n, p in enumerate(z_peers)
        ]

    def prefix_x():
        for copy in steps["z"]:
            copy.wait_recv()
        z_sum[...] = dp_ref[:, sixteen(me.z, 64)] + z_buf[0] + z_buf[1] + z_buf[2]
        steps["x"] = [
            start(z_sum.at[:, sixteen(lax.rem(me.x + n + 1, 4), 16)], px_buf.at[n], px_sem.at[n], p)
            for n, p in enumerate(x_peers)
        ]

    def prefix_y():
        for copy in steps["x"]:
            copy.wait_recv()
        piece = z_sum[:, sixteen(me.x, 16)] + px_buf[0] + px_buf[1] + px_buf[2]
        px_sum[...] = piece
        py_buf[me.y] = piece
        steps["y"] = [
            start(px_sum, py_buf.at[me.y], py_sem.at[n], p) for n, p in enumerate(y_peers)
        ]

    def prefix_ax():
        for copy in steps["y"]:
            copy.wait_recv()
        fin[me.z, me.x] = ((py_buf[0] + py_buf[1]) + py_buf[2]) + py_buf[3]
        block = fin.at[me.z, me.x]
        steps["ax"] = [start(block, block, ax_sem.at[n], p) for n, p in enumerate(x_peers)]

    def prefix_az():
        for copy in steps["ax"]:
            copy.wait_recv()
        block = fin.at[me.z]
        steps["az"] = [start(block, block, az_sem.at[n], p) for n, p in enumerate(z_peers)]

    def prefix_ac():
        for copy in steps["az"]:
            copy.wait_recv()
        steps["ac"] = start(fin, fin_other, ac_sem, sibling)

    def prefix_lay(src, which):
        at = lanes(which * wide, wide)
        for z in range(4):
            for x in range(4):
                rows = slice(z * 64 + x * 16, z * 64 + x * 16 + 16)
                dpk_ref[rows, at] = src[z, x, 0]
                dpv_ref[rows, at] = src[z, x, 1]

    gather_first(0)
    swaps = [
        start(src, dst, swap_sem.at[n], sibling)
        for n, (src, dst) in enumerate(
            (
                (q_hbm.at[:, lanes(other * HALF, HALF)], q_ref.at[1]),
                (g_hbm.at[:, lanes(other * HALF, HALF)], g_ref.at[1]),
                (norm_hbm.at[other16], table.at[1, 0]),
                (dot_hbm.at[other16], table.at[1, 1]),
            )
        )
    ]
    for copy in loads:
        copy.wait()
    gather_first(1)
    prefix_tile(0, 0)
    prefix_tile(0, 1)
    prefix_tile(1, 0)
    gather_second(0)
    prefix_tile(1, 1)
    for copy in swaps:
        copy.wait_recv()
    prefix_tile(0, 2)
    prefix_tile(0, 3)
    gather_second(1)
    gather_first(2)
    prefix_tile(1, 2)
    prefix_tile(1, 3)
    gather_third(0)
    prefix_z()
    gather_end(0)
    value_tile(0, 0)
    gather_third(1)
    value_tile(0, 1)
    gather_second(2)
    gather_first(3)
    value_tile(0, 2)
    prefix_x()
    value_tile(0, 3)
    reduce_first(1)
    gather_end(1)
    gather_third(2)
    key_tile(0, 0)
    gather_second(3)
    prefix_y()
    key_tile(0, 1)
    reduce_second(1)
    key_tile(0, 2)
    gather_third(3)
    prefix_ax()
    key_tile(0, 3)
    reduce_first(0)
    give_dq(0)
    gather_end(2)
    value_tile(1, 0)
    pass_on(1)
    value_tile(1, 1)
    reduce_second(0)
    prefix_az()
    value_tile(1, 2)
    value_tile(1, 3)
    reduce_first(3)
    gather_end(3)
    key_tile(1, 0)
    pass_on(0)
    reduce_last(1)
    prefix_ac()
    key_tile(1, 1)
    reduce_second(3)
    key_tile(1, 2)
    prefix_lay(fin, core)
    key_tile(1, 3)
    reduce_first(2)
    give_dq(1)
    pass_on(3)
    reduce_second(2)
    reduce_last(0)
    steps["ac"].wait_recv()
    prefix_lay(fin_other, other)
    pass_on(2)
    reduce_last(3)
    take_last(1)
    take_last(0)
    take_last(3)
    reduce_last(2)
    take_last(2)
    for copy in backs:
        copy.wait_recv()
    for copy in keeps:
        copy.wait()
    for copy in sent:
        copy.wait_send()


def run(index, plen, q, g, norm, dot, k, v, pk, pv):
    smem = pl.BlockSpec(memory_space=pltpu.SMEM)
    vmem = pl.BlockSpec(memory_space=pltpu.VMEM)
    anywhere = pl.BlockSpec(memory_space=pl.ANY)
    dma = pltpu.SemaphoreType.DMA
    unit = (ROWS, WIDTH)
    wide = HEADS * WIDTH
    return pl.pallas_call(
        fused_kernel,
        out_shape=(
            jax.ShapeDtypeStruct((ROWS, 2 * HALF), BF16),
            jax.ShapeDtypeStruct((ROWS, 2 * wide), BF16),
            jax.ShapeDtypeStruct((ROWS, 2 * wide), BF16),
            jax.ShapeDtypeStruct((PREFIX, 2 * wide), F32),
            jax.ShapeDtypeStruct((PREFIX, 2 * wide), F32),
        ),
        in_specs=[smem] * 2 + [anywhere] * 8,
        out_specs=(anywhere, vmem, vmem, vmem, vmem),
        scratch_shapes=[
            pltpu.VMEM((2, ROWS, HALF), BF16),
            pltpu.VMEM((2, ROWS, HALF), BF16),
            pltpu.VMEM((2, 2, 16, ROWS), F32),
            pltpu.VMEM((2, PREFIX, wide), BF16),
            pltpu.VMEM((16, 2, SPAN, WIDTH), BF16),
            pltpu.VMEM((16, 2, SPAN, WIDTH), BF16),
            pltpu.VMEM((16, 2, SPAN, WIDTH), BF16),
            pltpu.VMEM((16, 2, SPAN, WIDTH), BF16),
            pltpu.VMEM((2, REACH * SPAN, WIDTH), BF16),
            pltpu.VMEM((4, REACH * SPAN, LANES), F32),
            pltpu.VMEM((2, 4, REACH + 1, SPAN, WIDTH), F32),
            pltpu.VMEM((2, 4, REACH + 1, SPAN, WIDTH), F32),
            pltpu.VMEM((HEADS, 4, LANES, WIDTH), F32),
            pltpu.VMEM((2, ROWS, HALF), BF16),
            pltpu.VMEM((2, PREFIX, wide), F32),
            pltpu.VMEM((2, UNITS) + unit, BF16),
            pltpu.VMEM((2, UNITS) + unit, BF16),
            pltpu.VMEM((2, 2, UNITS) + unit, BF16),
            pltpu.VMEM((2, UNITS) + unit, BF16),
            pltpu.VMEM((2, UNITS) + unit, BF16),
            pltpu.VMEM((2, UNITS) + unit, BF16),
            pltpu.VMEM((2, 2, UNITS) + unit, BF16),
            pltpu.VMEM((2, UNITS) + unit, BF16),
            pltpu.VMEM((2, UNITS) + unit, BF16),
            pltpu.VMEM((2, UNITS) + unit, BF16),
            pltpu.VMEM((2, UNITS) + unit, BF16),
            pltpu.VMEM((2, UNITS) + unit, BF16),
            pltpu.VMEM((2, UNITS) + unit, F32),
            pltpu.VMEM((UNITS,) + unit, BF16),
            pltpu.VMEM((UNITS,) + unit, BF16),
            pltpu.VMEM((3, 2, 64, wide), F32),
            pltpu.VMEM((2, 64, wide), F32),
            pltpu.VMEM((3, 2, 16, wide), F32),
            pltpu.VMEM((2, 16, wide), F32),
            pltpu.VMEM((4, 2, 16, wide), F32),
            pltpu.VMEM((4, 4, 2, 16, wide), F32),
            pltpu.VMEM((4, 4, 2, 16, wide), F32),
            dma((6,)),
            dma((UNITS,)),
            dma((UNITS, 2)),
            dma((4, 2)),
            dma((2, 2, 2, UNITS, 2)),
            dma((2, 2, UNITS, 2)),
            dma((2, UNITS, 2)),
            dma((2, UNITS, 2)),
            dma((HEADS,)),
            dma((HEADS, 2)),
            dma((2, UNITS, 2)),
            dma((2, UNITS, 2)),
            dma((2, 2, UNITS, 2)),
            dma((2, UNITS, 2)),
            dma((2, UNITS, 2)),
            dma((2, UNITS, 2)),
            dma((UNITS, 2)),
            dma((3, 2)),
            dma((3, 2)),
            dma((3, 2)),
            dma((3, 2)),
            dma((3, 2)),
            dma((2,)),
        ],
        compiler_params=pltpu.CompilerParams(
            collective_id=0, has_side_effects=True, vmem_limit_bytes=60 * 1024 * 1024
        ),
        name="pack_grads",
    )(index, plen, q, g, norm, dot, k, v, pk, pv)


def copy_kernel(*refs):
    count = (len(refs) - 2) // 3
    ins, outs, held = refs[:count], refs[count : 2 * count], refs[2 * count : 3 * count]
    in_sem, out_sem = refs[-2:]
    parts = []
    for n in range(count):
        pieces = 4 if n == 0 else 1
        size = ins[n].shape[0] // pieces
        for part in range(pieces):
            parts.append((n, pl.ds(part * size, size)))
    first = [
        pltpu.make_async_copy(ins[n].at[rows], held[n].at[rows], in_sem.at[i])
        for i, (n, rows) in enumerate(parts)
    ]
    second = [
        pltpu.make_async_copy(held[n].at[rows], outs[n].at[rows], out_sem.at[i])
        for i, (n, rows) in enumerate(parts)
    ]
    for copy in first:
        copy.start()
    for copy, onward in zip(first, second):
        copy.wait()
        onward.start()
    for copy in second:
        copy.wait()


def settle(arrays):
    anywhere = pl.BlockSpec(memory_space=pl.ANY)
    return pl.pallas_call(
        copy_kernel,
        out_shape=tuple(jax.ShapeDtypeStruct(a.shape, a.dtype) for a in arrays),
        in_specs=[anywhere] * len(arrays),
        out_specs=(anywhere,) * len(arrays),
        scratch_shapes=[pltpu.VMEM(a.shape, a.dtype) for a in arrays]
        + [pltpu.SemaphoreType.DMA((len(arrays) + 3,)), pltpu.SemaphoreType.DMA((len(arrays) + 3,))],
        name="results",
    )(*arrays)


def local(
    query_matrix,
    key_matrix,
    value_matrix,
    output_gradient,
    log_softmax_norm,
    output_dot_rows,
    shared_prefix_keys,
    shared_prefix_values,
    prefix_len,
    segments,
    span_order,
):
    results = run(
        prepare(span_order[0], segments),
        prefix_len,
        query_matrix[0],
        output_gradient[0],
        log_softmax_norm[0],
        output_dot_rows[0],
        key_matrix.reshape(2, SPAN, KEY_VALUE_HEADS * WIDTH),
        value_matrix.reshape(2, SPAN, KEY_VALUE_HEADS * WIDTH),
        shared_prefix_keys,
        shared_prefix_values,
    )
    dq, dk, dv, dpk, dpv = settle(results)
    return dq[None], dk[None], dv[None], dpk, dpv


def solution(mesh):
    return jax.shard_map(
        local,
        mesh=mesh,
        in_specs=(
            P("dp", "blk", None),
            P("dp", "blk", None),
            P("dp", "blk", None),
            P("dp", "blk", None),
            P("dp", None, "blk"),
            P("dp", None, "blk"),
            P(),
            P(),
            P("dp"),
            P("dp", None),
            P("dp", None),
        ),
        out_specs=(P("dp", "blk", None), P("dp", "blk", None), P("dp", "blk", None), P(), P()),
        check_vma=False,
    )
```

time: 474 us -> 82 us (0.17)
  waiting for transfers between devices: 415 us -> 0 us
  Pallas kernels: 31.9 us -> 80.3 us
  between operations: 14.5 us -> 1.47 us
  local copies, waits for them, and re-layouts: 10.2 us -> 0 us
    reduce_scatter x2 -> x0, waiting for transfers between devices: 155 us -> none  [the longest x1 79.1 us: local(): dv = lax.psum_scatter(dv, 'blk', scatter_dimension=0, tiled=True)]
    psum x1 -> x0, waiting for transfers between devices: 154 us -> none  [local(): prefix = lax.psum(jnp.stack([dpk, dpv]), ('dp', 'blk'))]
    all_gather x2 -> x0, waiting for transfers between devices: 104 us -> none  [the longest x1 51.9 us: local(): values = lax.all_gather(value_matrix[0], 'blk', axis=0, tiled=True)]
    pallas_call x1 -> x3, Pallas kernels: 31.9 us -> 80.3 us  [the longest x1 75.8 us: run(): pl.pallas_call(fused_kernel, out_shape=(jax.ShapeDtypeStruct((ROWS, 2 * H...]
    unnamed x10 -> x0, local copies, waits for them, and re-layouts: 5.37 us -> none
  transfers between devices with their start and end apart: 5 -> 0, of which waited for: 5 -> 0; matrix products, arithmetic and copies ran while one was open for 1% -> 0% of each run, Pallas kernels for 0% -> 0%
where the time goes in v3:
time: 82 us; the launch traced here: 81.8 us
  Pallas kernels  80.3 us (98%)
  between operations  1.47 us (2%)
    pallas_call x1, Pallas kernels, run(): pl.pallas_call(fused_kernel, out_shape=(jax.ShapeDtypeStruct((ROWS, 2 * H...  75.8 us
    pallas_call x1, Pallas kernels, settle(): pl.pallas_call(copy_kernel, out_shape=tuple((jax.ShapeDtypeStruct(a.shape...  2.75 us
    pallas_call x1, Pallas kernels, prepare(): pl.pallas_call(prepare_kernel, out_shape=jax.ShapeDtypeStruct((256,), jnp...  1.76 us

profile of v3, /device:TPU:1, one launch (start us, length us, event | category | flops | bytes accessed | tf_op | source)
XLA Modules:
  0.0 81.8 jit_solution(6636302897608586354)
XLA Ops:
  1.3 1.8 %tables.1.index_ref = s32[256]{0:T(256)} custom-call(s32[32]{0:T(128)} %bitcast.16, s32[1,3072]{1,0:T(1,128)} %segments_ref.1), custom_call_target="tpu_custom_call" | custom-call | tf_op jit(solution)/shard_map/tables/pallas_call | solution.py:109
  3.0 75.8 %pack_grads.1 = (bf16[192,4096]{1,0:T(8,128)(2,1)}, bf16[192,512]{1,0:T(8,128)(2,1)}, bf16[192,512]{1,0:T(8,128)(2,1)}, f32[256,512]{1,0:T(8,128)}, f32[256,512]{1,0:T(8,128)}) custom-call(s32[256]{0:T(256)} %tables.1.index_ref, s32[1]{0:T(128)S(6)} %copy.16.plen_ref, bf16[192,4096]{1,0:T(8,128)(2,1)} %bitcast.10, bf16[192,4096]{1,0:T(8,128)(2,1)} %bitcast.11, ...), custom_call_target="tpu_custom_call" | custom-call | tf_op jit(solution)/shard_map/pack_grads/pallas_call | solution.py:647
  78.9 2.7 %results.1 = (bf16[192,4096]{1,0:T(8,128)(2,1)}, bf16[192,512]{1,0:T(8,128)(2,1)}, bf16[192,512]{1,0:T(8,128)(2,1)}, f32[256,512]{1,0:T(8,128)}, f32[256,512]{1,0:T(8,128)}) custom-call(bf16[192,4096]{1,0:T(8,128)(2,1)} %get-tuple-element.15.refs_0_, bf16[192,512]{1,0:T(8,128)(2,1)} %get-tuple-element.16.refs_1_, ...), custom_call_target="tpu_custom_call" | custom-call | tf_op jit(solution)/shard_map/results/pallas_call | solution.py:756

commit v4 on v3

--- a/solution.py
+++ b/solution.py
@@ -21,6 +21,7 @@
 STARTS, PLACES, BLOCKS, HALVES, SLOTS = 0, 8, 16, 64, 128
 HEADS = 2
 UNITS = 2 * HEADS
+DIRECT_GATHER, DIRECT_REDUCE = (0, 1, 2, 3), (0, 1, 2, 3)
 HALF = HEADS * GROUP * WIDTH
 SCALE = WIDTH**-0.5
 LOG2E = 1.4426950408889634
@@ -197,7 +198,7 @@
     core, other = me.core, 1 - me.core
     mine = me.chip(0, 0)
     sibling = me.at(other=True)
-    up, down, across = me.at(dy=1), me.at(dy=3), me.at(dx=2)
+    up, down, opposite, across = me.at(dy=1), me.at(dy=3), me.at(dy=2), me.at(dx=2)
     z_peers = [me.at(dz=d) for d in (1, 2, 3)]
     x_peers = [me.at(dx=d) for d in (1, 2, 3)]
     y_peers = [me.at(dy=d) for d in (1, 2, 3)]
@@ -264,6 +265,8 @@
             block = kv[u].at[mine * 2 + r]
             gx_copies[rr, u] = start(block, block, gx_sem.at[rr, u], across)
             y_pair(0, rr, u, r)
+            if u in DIRECT_GATHER:
+                f_copies[rr, 0, u] = start(block, block, f_sem.at[rr, 0, u], opposite)
 
     def forward(col, u):
         for d, (rr, dy, peer) in enumerate(((0, 3, up), (1, 1, down))):
@@ -275,7 +278,8 @@
         for rr, r in enumerate((core, other)):
             gx_copies[rr, u].wait_recv()
             y_pair(1, rr, u, r)
-        forward(0, u)
+        if u not in DIRECT_GATHER:
+            forward(0, u)
 
     def gather_third(u):
         for rr, r in enumerate((core, other)):
@@ -286,6 +290,9 @@
     def gather_end(u):
         y_copies[0, 1, u][0].wait_recv()
         y_copies[0, 0, u][1].wait_recv()
+        if u in DIRECT_GATHER:
+            y_copies[0, 0, u][0].wait_recv()
+            y_copies[0, 1, u][1].wait_recv()
         for rr in range(2):
             for d in range(2):
                 y_copies[1, rr, u][d].wait_recv()
@@ -424,16 +431,23 @@
                 far_out[d, u, at] = (
                     own_part(u, me.chip(2, 0), r, n) + xf_buf[r, u, at].astype(F32)
                 ).astype(BF16)
-            far[d, u] = start(far_out.at[d, u], a_buf.at[d, u], a_sem.at[d, u], peer)
+            to = opposite if u in DIRECT_REDUCE else peer
+            far[d, u] = start(far_out.at[d, u], a_buf.at[d, u], a_sem.at[d, u], to)
+
+    def send_mid(u):
+        for d, (peer, dy) in ways:
+            if u not in DIRECT_REDUCE:
+                far[d, u].wait_recv()
+            for n, at in pieces:
+                value = own_part(u, me.chip(dy, 0), 1 - d, n)
+                if u not in DIRECT_REDUCE:
+                    value = value + a_buf[d, u, at].astype(F32)
+                c_out[d, u, at] = value.astype(BF16)
+            mid[d, u] = start(c_out.at[d, u], c_buf.at[d, u], c_sem.at[d, u], peer)
 
     def pass_on(u):
-        for d, (peer, dy) in ways:
-            far[d, u].wait_recv()
-            for n, at in pieces:
-                c_out[d, u, at] = (
-                    own_part(u, me.chip(dy, 0), 1 - d, n) + a_buf[d, u, at].astype(F32)
-                ).astype(BF16)
-            mid[d, u] = start(c_out.at[d, u], c_buf.at[d, u], c_sem.at[d, u], peer)
+        if u not in DIRECT_REDUCE:
+            send_mid(u)
 
     def over_x(u):
         for r in range(2):
@@ -452,12 +466,17 @@
             d = 1 - r
             mid[d, u].wait_recv()
             near[1 - d, u].wait_recv()
+            if u in DIRECT_REDUCE:
+                far[d, u].wait_recv()
             for n, at in pieces:
-                held[r, u, at] = (
+                value = (
                     own_part(u, mine, r, n)
                     + c_buf[d, u, at].astype(F32)
                     + b_buf[1 - d, u, at].astype(F32)
                 )
+                if u in DIRECT_REDUCE:
+                    value = value + a_buf[d, u, at].astype(F32)
+                held[r, u, at] = value
 
     def finish(u):
         for r in range(2):
@@ -478,6 +497,8 @@
         send_cross(u)
         send_edge(u)
         send_near(u)
+        if u in DIRECT_REDUCE:
+            send_mid(u)
 
     def reduce_second(u):
         send_far(u)
@@ -562,72 +583,72 @@
     prefix_tile(0, 1)
     prefix_tile(1, 0)
     gather_second(0)
+    gather_first(2)
     prefix_tile(1, 1)
     for copy in swaps:
         copy.wait_recv()
     prefix_tile(0, 2)
+    gather_third(0)
+    gather_second(1)
+    gather_first(3)
     prefix_tile(0, 3)
-    gather_second(1)
-    gather_first(2)
     prefix_tile(1, 2)
     prefix_tile(1, 3)
-    gather_third(0)
     prefix_z()
     gather_end(0)
     value_tile(0, 0)
     gather_third(1)
     value_tile(0, 1)
     gather_second(2)
-    gather_first(3)
     value_tile(0, 2)
-    prefix_x()
     value_tile(0, 3)
     reduce_first(1)
+    gather_second(3)
+    gather_third(2)
     gather_end(1)
-    gather_third(2)
     key_tile(0, 0)
-    gather_second(3)
-    prefix_y()
+    prefix_x()
     key_tile(0, 1)
+    gather_third(3)
+    key_tile(0, 2)
     reduce_second(1)
-    key_tile(0, 2)
-    gather_third(3)
-    prefix_ax()
     key_tile(0, 3)
     reduce_first(0)
     give_dq(0)
+    prefix_y()
     gather_end(2)
     value_tile(1, 0)
+    value_tile(1, 1)
     pass_on(1)
-    value_tile(1, 1)
+    value_tile(1, 2)
     reduce_second(0)
-    prefix_az()
-    value_tile(1, 2)
     value_tile(1, 3)
     reduce_first(3)
+    prefix_ax()
     gather_end(3)
     key_tile(1, 0)
     pass_on(0)
+    key_tile(1, 1)
     reduce_last(1)
-    prefix_ac()
-    key_tile(1, 1)
-    reduce_second(3)
     key_tile(1, 2)
-    prefix_lay(fin, core)
+    prefix_az()
     key_tile(1, 3)
     reduce_first(2)
     give_dq(1)
-    pass_on(3)
+    reduce_second(3)
+    prefix_ac()
     reduce_second(2)
     reduce_last(0)
+    pass_on(3)
+    take_last(1)
+    take_last(0)
+    prefix_lay(fin, core)
+    pass_on(2)
+    reduce_last(3)
     steps["ac"].wait_recv()
     prefix_lay(fin_other, other)
-    pass_on(2)
-    reduce_last(3)
-    take_last(1)
-    take_last(0)
+    reduce_last(2)
     take_last(3)
-    reduce_last(2)
     take_last(2)
     for copy in backs:
         copy.wait_recv()
@@ -698,7 +719,7 @@
             dma((UNITS, 2)),
             dma((4, 2)),
             dma((2, 2, 2, UNITS, 2)),
-            dma((2, 2, UNITS, 2)),
+            dma((2, 1, UNITS, 2)),
             dma((2, UNITS, 2)),
             dma((2, UNITS, 2)),
             dma((HEADS,)),

time: 82 us -> 77.4 us (0.944)
  Pallas kernels: 80.3 us -> 75.7 us
    pallas_call x1, Pallas kernels: 75.8 us -> 71.2 us  [run(): pl.pallas_call(fused_kernel, out_shape=(jax.ShapeDtypeStruct((ROWS, 2 * H...]
where the time goes in v4:
time: 77.4 us; the launch traced here: 77.1 us
  Pallas kernels  75.7 us (98%)
  between operations  1.47 us (2%)
    pallas_call x1, Pallas kernels, run(): pl.pallas_call(fused_kernel, out_shape=(jax.ShapeDtypeStruct((ROWS, 2 * H...  71.2 us
    pallas_call x1, Pallas kernels, settle(): pl.pallas_call(copy_kernel, out_shape=tuple((jax.ShapeDtypeStruct(a.shape...  2.75 us
    pallas_call x1, Pallas kernels, prepare(): pl.pallas_call(prepare_kernel, out_shape=jax.ShapeDtypeStruct((256,), jnp...  1.76 us

profile of v4, /device:TPU:1, one launch (start us, length us, event | category | flops | bytes accessed | tf_op | source)
XLA Modules:
  0.0 77.1 jit_solution(8333755865936642564)
XLA Ops:
  1.3 1.8 %tables.1.index_ref = s32[256]{0:T(256)} custom-call(s32[32]{0:T(128)} %bitcast.16, s32[1,3072]{1,0:T(1,128)} %segments_ref.1), custom_call_target="tpu_custom_call" | custom-call | tf_op jit(solution)/shard_map/tables/pallas_call | solution.py:110
  3.0 71.2 %pack_grads.1 = (bf16[192,4096]{1,0:T(8,128)(2,1)}, bf16[192,512]{1,0:T(8,128)(2,1)}, bf16[192,512]{1,0:T(8,128)(2,1)}, f32[256,512]{1,0:T(8,128)}, f32[256,512]{1,0:T(8,128)}) custom-call(s32[256]{0:T(256)} %tables.1.index_ref, s32[1]{0:T(128)S(6)} %copy.16.plen_ref, bf16[192,4096]{1,0:T(8,128)(2,1)} %bitcast.10, bf16[192,4096]{1,0:T(8,128)(2,1)} %bitcast.11, ...), custom_call_target="tpu_custom_call" | custom-call | tf_op jit(solution)/shard_map/pack_grads/pallas_call | solution.py:668
  74.2 2.7 %results.1 = (bf16[192,4096]{1,0:T(8,128)(2,1)}, bf16[192,512]{1,0:T(8,128)(2,1)}, bf16[192,512]{1,0:T(8,128)(2,1)}, f32[256,512]{1,0:T(8,128)}, f32[256,512]{1,0:T(8,128)}) custom-call(bf16[192,4096]{1,0:T(8,128)(2,1)} %get-tuple-element.15.refs_0_, bf16[192,512]{1,0:T(8,128)(2,1)} %get-tuple-element.16.refs_1_, ...), custom_call_target="tpu_custom_call" | custom-call | tf_op jit(solution)/shard_map/results/pallas_call | solution.py:777

commit v5 on v4

--- a/solution.py
+++ b/solution.py
@@ -21,7 +21,7 @@
 STARTS, PLACES, BLOCKS, HALVES, SLOTS = 0, 8, 16, 64, 128
 HEADS = 2
 UNITS = 2 * HEADS
-DIRECT_GATHER, DIRECT_REDUCE = (0, 1, 2, 3), (0, 1, 2, 3)
+SPLIT = (0,)
 HALF = HEADS * GROUP * WIDTH
 SCALE = WIDTH**-0.5
 LOG2E = 1.4426950408889634
@@ -155,12 +155,9 @@
     a_buf,
     b_buf,
     e_buf,
-    c_buf,
-    c_out,
     x_buf,
     x_out,
     xf_buf,
-    held,
     last_out,
     last_buf,
     z_buf,
@@ -183,7 +180,6 @@
     a_sem,
     b_sem,
     e_sem,
-    c_sem,
     x_sem,
     xf_sem,
     last_sem,
@@ -252,51 +248,43 @@
 
     y_copies, gx_copies, f_copies, gf_copies = {}, {}, {}, {}
 
-    def y_pair(col, rr, u, r):
-        block = kv[u].at[me.chip(0, col) * 2 + r]
+    def parts(u):
+        return ((0, core), (1, other)) if u in SPLIT else ((0, None),)
+
+    def view(u, chip, r):
+        at = pl.ds(chip * 2, 2) if r is None else pl.ds(chip * 2 + r, 1)
+        return kv[u].at[at]
+
+    def y_pair(col, rr, u, block):
         y_copies[col, rr, u] = [
             start(block, block, y_sem.at[d, col, rr, u], peer) for d, peer in enumerate((up, down))
         ]
 
     def gather_first(u):
-        for rr, r in enumerate((core, other)):
-            if rr == 1:
+        for rr, r in parts(u):
+            if rr == 1 or r is None:
                 pair[u].wait_recv()
-            block = kv[u].at[mine * 2 + r]
+            block = view(u, mine, r)
             gx_copies[rr, u] = start(block, block, gx_sem.at[rr, u], across)
-            y_pair(0, rr, u, r)
-            if u in DIRECT_GATHER:
-                f_copies[rr, 0, u] = start(block, block, f_sem.at[rr, 0, u], opposite)
-
-    def forward(col, u):
-        for d, (rr, dy, peer) in enumerate(((0, 3, up), (1, 1, down))):
-            y_copies[col, rr, u][d].wait_recv()
-            block = kv[u].at[me.chip(dy, col) * 2 + (core if rr == 0 else other)]
-            f_copies[d, col, u] = start(block, block, f_sem.at[d, col, u], peer)
+            f_copies[rr, u] = start(block, block, f_sem.at[rr, u], opposite)
+            y_pair(0, rr, u, block)
 
     def gather_second(u):
-        for rr, r in enumerate((core, other)):
+        for rr, r in parts(u):
             gx_copies[rr, u].wait_recv()
-            y_pair(1, rr, u, r)
-        if u not in DIRECT_GATHER:
-            forward(0, u)
+            y_pair(1, rr, u, view(u, me.chip(0, 1), r))
 
     def gather_third(u):
-        for rr, r in enumerate((core, other)):
-            f_copies[rr, 0, u].wait_recv()
-            block = kv[u].at[me.chip(2, 0) * 2 + r]
+        for rr, r in parts(u):
+            f_copies[rr, u].wait_recv()
+            block = view(u, me.chip(2, 0), r)
             gf_copies[rr, u] = start(block, block, gf_sem.at[rr, u], across)
 
     def gather_end(u):
-        y_copies[0, 1, u][0].wait_recv()
-        y_copies[0, 0, u][1].wait_recv()
-        if u in DIRECT_GATHER:
-            y_copies[0, 0, u][0].wait_recv()
-            y_copies[0, 1, u][1].wait_recv()
-        for rr in range(2):
-            for d in range(2):
-                y_copies[1, rr, u][d].wait_recv()
-        for rr in range(2):
+        for rr, r in parts(u):
+            for col in range(2):
+                for d in range(2):
+                    y_copies[col, rr, u][d].wait_recv()
             gf_copies[rr, u].wait_recv()
 
     lane_row = lax.rem(lax.broadcasted_iota(jnp.int32, (1, LANES), 1), SPAN)
@@ -398,95 +386,64 @@
             total = term if total is None else total + term
         return total
 
-    pieces = [(n, slice(n * SPAN, (n + 1) * SPAN)) for n in range(2)]
+    pieces = [(r, n, slice(n * SPAN, (n + 1) * SPAN)) for r in range(2) for n in range(2)]
     ways = tuple(enumerate(((up, 1), (down, 3))))
-    cross, edge, near, far, mid, over, last = {}, {}, {}, {}, {}, {}, {}
+    cross, edge, near, far, over, last = {}, {}, {}, {}, {}, {}
 
     def send_cross(u):
-        for r in range(2):
-            for n, at in pieces:
-                xf_out[r, u, at] = own_part(u, me.chip(2, 1), r, n).astype(BF16)
-            cross[r, u] = start(xf_out.at[r, u], xf_buf.at[r, u], xf_sem.at[r, u], across)
+        for r, n, at in pieces:
+            xf_out[u, r, at] = own_part(u, me.chip(2, 1), r, n).astype(BF16)
+        cross[u] = start(xf_out.at[u], xf_buf.at[u], xf_sem.at[u], across)
 
     def send_edge(u):
-        for r in range(2):
-            for d, (peer, dy) in ways:
-                for n, at in pieces:
-                    edge_out[d, r, u, at] = own_part(u, me.chip(dy, 1), r, n).astype(BF16)
-                edge[d, r, u] = start(
-                    edge_out.at[d, r, u], e_buf.at[d, r, u], e_sem.at[d, r, u], peer
-                )
+        for d, (peer, dy) in ways:
+            for r, n, at in pieces:
+                edge_out[d, u, r, at] = own_part(u, me.chip(dy, 1), r, n).astype(BF16)
+            edge[d, u] = start(edge_out.at[d, u], e_buf.at[d, u], e_sem.at[d, u], peer)
 
     def send_near(u):
         for d, (peer, dy) in ways:
-            for n, at in pieces:
-                near_out[d, u, at] = own_part(u, me.chip(dy, 0), d, n).astype(BF16)
+            for r, n, at in pieces:
+                near_out[d, u, r, at] = own_part(u, me.chip(dy, 0), r, n).astype(BF16)
             near[d, u] = start(near_out.at[d, u], b_buf.at[d, u], b_sem.at[d, u], peer)
 
     def send_far(u):
-        for d, (peer, dy) in ways:
-            r = 1 - d
-            cross[r, u].wait_recv()
-            for n, at in pieces:
-                far_out[d, u, at] = (
-                    own_part(u, me.chip(2, 0), r, n) + xf_buf[r, u, at].astype(F32)
-                ).astype(BF16)
-            to = opposite if u in DIRECT_REDUCE else peer
-            far[d, u] = start(far_out.at[d, u], a_buf.at[d, u], a_sem.at[d, u], to)
-
-    def send_mid(u):
-        for d, (peer, dy) in ways:
-            if u not in DIRECT_REDUCE:
-                far[d, u].wait_recv()
-            for n, at in pieces:
-                value = own_part(u, me.chip(dy, 0), 1 - d, n)
-                if u not in DIRECT_REDUCE:
-                    value = value + a_buf[d, u, at].astype(F32)
-                c_out[d, u, at] = value.astype(BF16)
-            mid[d, u] = start(c_out.at[d, u], c_buf.at[d, u], c_sem.at[d, u], peer)
-
-    def pass_on(u):
-        if u not in DIRECT_REDUCE:
-            send_mid(u)
+        cross[u].wait_recv()
+        for r, n, at in pieces:
+            far_out[u, r, at] = (
+                own_part(u, me.chip(2, 0), r, n) + xf_buf[u, r, at].astype(F32)
+            ).astype(BF16)
+        far[u] = start(far_out.at[u], a_buf.at[u], a_sem.at[u], opposite)
 
     def over_x(u):
-        for r in range(2):
-            for d in range(2):
-                edge[d, r, u].wait_recv()
-            for n, at in pieces:
-                x_out[r, u, at] = (
-                    own_part(u, me.chip(0, 1), r, n)
-                    + e_buf[0, r, u, at].astype(F32)
-                    + e_buf[1, r, u, at].astype(F32)
-                ).astype(BF16)
-            over[r, u] = start(x_out.at[r, u], x_buf.at[r, u], x_sem.at[r, u], across)
-
-    def hold(u):
-        for r in range(2):
-            d = 1 - r
-            mid[d, u].wait_recv()
-            near[1 - d, u].wait_recv()
-            if u in DIRECT_REDUCE:
-                far[d, u].wait_recv()
-            for n, at in pieces:
-                value = (
-                    own_part(u, mine, r, n)
-                    + c_buf[d, u, at].astype(F32)
-                    + b_buf[1 - d, u, at].astype(F32)
-                )
-                if u in DIRECT_REDUCE:
-                    value = value + a_buf[d, u, at].astype(F32)
-                held[r, u, at] = value
-
-    def finish(u):
-        for r in range(2):
-            over[r, u].wait_recv()
-        last_out[u] = (held[other, u] + x_buf[other, u].astype(F32)).astype(BF16)
+        for d in range(2):
+            edge[d, u].wait_recv()
+        for r, n, at in pieces:
+            x_out[u, r, at] = (
+                own_part(u, me.chip(0, 1), r, n)
+                + e_buf[0, u, r, at].astype(F32)
+                + e_buf[1, u, r, at].astype(F32)
+            ).astype(BF16)
+        over[u] = start(x_out.at[u], x_buf.at[u], x_sem.at[u], across)
+
+    def whole_sum(u, r, n, at):
+        return (
+            own_part(u, mine, r, n)
+            + b_buf[0, u, r, at].astype(F32)
+            + b_buf[1, u, r, at].astype(F32)
+            + a_buf[u, r, at].astype(F32)
+            + x_buf[u, r, at].astype(F32)
+        ).astype(BF16)
+
+    def reduce_last(u):
+        for copy in (near[0, u], near[1, u], far[u], over[u]):
+            copy.wait_recv()
+        for r, n, at in pieces[:2]:
+            last_out[u, at] = whole_sum(u, other, n, at)
         last[u] = start(last_out.at[u], last_buf.at[u], last_sem.at[u], sibling)
         ref = (dk_ref, dv_ref)[u % 2]
-        ref[:, lanes((core * 2 + u // 2) * WIDTH, WIDTH)] = (
-            held[core, u] + x_buf[core, u].astype(F32)
-        ).astype(BF16)
+        for r, n, at in pieces[:2]:
+            ref[at, lanes((core * 2 + u // 2) * WIDTH, WIDTH)] = whole_sum(u, core, n, at)
 
     def take_last(u):
         last[u].wait_recv()
@@ -497,16 +454,10 @@
         send_cross(u)
         send_edge(u)
         send_near(u)
-        if u in DIRECT_REDUCE:
-            send_mid(u)
 
     def reduce_second(u):
         send_far(u)
         over_x(u)
-
-    def reduce_last(u):
-        hold(u)
-        finish(u)
 
     def sixteen(i, size):
         return pl.ds(pl.multiple_of(i * size, size), size)
@@ -599,18 +550,18 @@
     value_tile(0, 0)
     gather_third(1)
     value_tile(0, 1)
+    value_tile(0, 2)
     gather_second(2)
-    value_tile(0, 2)
     value_tile(0, 3)
     reduce_first(1)
     gather_second(3)
-    gather_third(2)
     gather_end(1)
     key_tile(0, 0)
+    gather_third(2)
     prefix_x()
     key_tile(0, 1)
+    key_tile(0, 2)
     gather_third(3)
-    key_tile(0, 2)
     reduce_second(1)
     key_tile(0, 3)
     reduce_first(0)
@@ -619,31 +570,27 @@
     gather_end(2)
     value_tile(1, 0)
     value_tile(1, 1)
-    pass_on(1)
+    reduce_second(0)
     value_tile(1, 2)
-    reduce_second(0)
     value_tile(1, 3)
     reduce_first(3)
     prefix_ax()
     gather_end(3)
     key_tile(1, 0)
-    pass_on(0)
+    reduce_last(1)
     key_tile(1, 1)
-    reduce_last(1)
     key_tile(1, 2)
+    reduce_second(3)
     prefix_az()
     key_tile(1, 3)
     reduce_first(2)
     give_dq(1)
-    reduce_second(3)
     prefix_ac()
     reduce_second(2)
     reduce_last(0)
-    pass_on(3)
     take_last(1)
     take_last(0)
     prefix_lay(fin, core)
-    pass_on(2)
     reduce_last(3)
     steps["ac"].wait_recv()
     prefix_lay(fin_other, other)
@@ -692,19 +639,16 @@
             pltpu.VMEM((HEADS, 4, LANES, WIDTH), F32),
             pltpu.VMEM((2, ROWS, HALF), BF16),
             pltpu.VMEM((2, PREFIX, wide), F32),
-            pltpu.VMEM((2, UNITS) + unit, BF16),
-            pltpu.VMEM((2, UNITS) + unit, BF16),
-            pltpu.VMEM((2, 2, UNITS) + unit, BF16),
-            pltpu.VMEM((2, UNITS) + unit, BF16),
-            pltpu.VMEM((2, UNITS) + unit, BF16),
-            pltpu.VMEM((2, UNITS) + unit, BF16),
-            pltpu.VMEM((2, 2, UNITS) + unit, BF16),
-            pltpu.VMEM((2, UNITS) + unit, BF16),
-            pltpu.VMEM((2, UNITS) + unit, BF16),
-            pltpu.VMEM((2, UNITS) + unit, BF16),
-            pltpu.VMEM((2, UNITS) + unit, BF16),
-            pltpu.VMEM((2, UNITS) + unit, BF16),
-            pltpu.VMEM((2, UNITS) + unit, F32),
+            pltpu.VMEM((UNITS, 2) + unit, BF16),
+            pltpu.VMEM((2, UNITS, 2) + unit, BF16),
+            pltpu.VMEM((2, UNITS, 2) + unit, BF16),
+            pltpu.VMEM((UNITS, 2) + unit, BF16),
+            pltpu.VMEM((UNITS, 2) + unit, BF16),
+            pltpu.VMEM((2, UNITS, 2) + unit, BF16),
+            pltpu.VMEM((2, UNITS, 2) + unit, BF16),
+            pltpu.VMEM((UNITS, 2) + unit, BF16),
+            pltpu.VMEM((UNITS, 2) + unit, BF16),
+            pltpu.VMEM((UNITS, 2) + unit, BF16),
             pltpu.VMEM((UNITS,) + unit, BF16),
             pltpu.VMEM((UNITS,) + unit, BF16),
             pltpu.VMEM((3, 2, 64, wide), F32),
@@ -719,17 +663,16 @@
             dma((UNITS, 2)),
             dma((4, 2)),
             dma((2, 2, 2, UNITS, 2)),
-            dma((2, 1, UNITS, 2)),
+            dma((2, UNITS, 2)),
             dma((2, UNITS, 2)),
             dma((2, UNITS, 2)),
             dma((HEADS,)),
             dma((HEADS, 2)),
+            dma((UNITS, 2)),
             dma((2, UNITS, 2)),
             dma((2, UNITS, 2)),
-            dma((2, 2, UNITS, 2)),
-            dma((2, UNITS, 2)),
-            dma((2, UNITS, 2)),
-            dma((2, UNITS, 2)),
+            dma((UNITS, 2)),
+            dma((UNITS, 2)),
             dma((UNITS, 2)),
             dma((3, 2)),
             dma((3, 2)),

time: 77.4 us -> 75.9 us (0.981)
  Pallas kernels: 75.7 us -> 74.2 us
    pallas_call x1, Pallas kernels: 71.2 us -> 69.7 us  [run(): pl.pallas_call(fused_kernel, out_shape=(jax.ShapeDtypeStruct((ROWS, 2 * H...]
where the time goes in v5:
time: 75.9 us; the launch traced here: 75.7 us
  Pallas kernels  74.2 us (98%)
  between operations  1.47 us (2%)
    pallas_call x1, Pallas kernels, run(): pl.pallas_call(fused_kernel, out_shape=(jax.ShapeDtypeStruct((ROWS, 2 * H...  69.7 us
    pallas_call x1, Pallas kernels, settle(): pl.pallas_call(copy_kernel, out_shape=tuple((jax.ShapeDtypeStruct(a.shape...  2.75 us
    pallas_call x1, Pallas kernels, prepare(): pl.pallas_call(prepare_kernel, out_shape=jax.ShapeDtypeStruct((256,), jnp...  1.76 us

profile of v5, /device:TPU:1, one launch (start us, length us, event | category | flops | bytes accessed | tf_op | source)
XLA Modules:
  0.0 75.7 jit_solution(130189082465390508)
XLA Ops:
  1.3 1.8 %tables.1.index_ref = s32[256]{0:T(256)} custom-call(s32[32]{0:T(128)} %bitcast.16, s32[1,3072]{1,0:T(1,128)} %segments_ref.1), custom_call_target="tpu_custom_call" | custom-call | tf_op jit(solution)/shard_map/tables/pallas_call | solution.py:110
  3.0 69.7 %pack_grads.1 = (bf16[192,4096]{1,0:T(8,128)(2,1)}, bf16[192,512]{1,0:T(8,128)(2,1)}, bf16[192,512]{1,0:T(8,128)(2,1)}, f32[256,512]{1,0:T(8,128)}, f32[256,512]{1,0:T(8,128)}) custom-call(s32[256]{0:T(256)} %tables.1.index_ref, s32[1]{0:T(128)S(6)} %copy.16.plen_ref, bf16[192,4096]{1,0:T(8,128)(2,1)} %bitcast.10, bf16[192,4096]{1,0:T(8,128)(2,1)} %bitcast.11, ...), custom_call_target="tpu_custom_call" | custom-call | tf_op jit(solution)/shard_map/pack_grads/pallas_call | solution.py:615
  72.8 2.7 %results.1 = (bf16[192,4096]{1,0:T(8,128)(2,1)}, bf16[192,512]{1,0:T(8,128)(2,1)}, bf16[192,512]{1,0:T(8,128)(2,1)}, f32[256,512]{1,0:T(8,128)}, f32[256,512]{1,0:T(8,128)}) custom-call(bf16[192,4096]{1,0:T(8,128)(2,1)} %get-tuple-element.15.refs_0_, bf16[192,512]{1,0:T(8,128)(2,1)} %get-tuple-element.16.refs_1_, ...), custom_call_target="tpu_custom_call" | custom-call | tf_op jit(solution)/shard_map/results/pallas_call | solution.py:720
